TPU v7x, 256 devices: a whole 4x4x8 slice. The times are simulated.
256 devices in a mesh: ctx: 64 (over x, z, core), head: 4 (over y).
Axes of the slice: x: 4, y: 4, z: 8, core: 2. Of those that a mesh axis runs over, the one named last changes fastest.
Arguments:
- queries: bfloat16 [8192, 4096], P('ctx', 'head'), may hold values from -100 to 100
- keys: bfloat16 [8192, 1024], P('ctx', 'head'), may hold values from -5 to 5
- values: bfloat16 [8192, 1024], P('ctx', 'head'), may hold values from -6 to 6
- grad_attn: bfloat16 [8192, 4096], P('ctx', 'head'), may hold values from -6 to 6
- ssm_input: bfloat16 [8192, 4096], P('ctx', 'head'), may hold values from -6 to 6
- ssm_b: bfloat16 [8192, 256], P('ctx'), may hold values from -0.375 to 0.375
- ssm_c: bfloat16 [8192, 256], P('ctx'), may hold values from -0.375 to 0.375
- log_decay: float32 [64, 8192], P('head', 'ctx'), may hold values from -1 to 0
- skip_gain: float32 [64], P('head'), may hold values from 0.5 to 1.5
- grad_ssm: bfloat16 [8192, 4096], P('ctx', 'head'), may hold values from -6 to 6
- doc_lengths: int32 [32], replicated, may hold values from 1 to 512, 8192 in all
Outputs:
- grad_queries: bfloat16 [8192, 4096], P('ctx', 'head')
- grad_keys: bfloat16 [8192, 1024], P('ctx', 'head')
- grad_values: bfloat16 [8192, 1024], P('ctx', 'head')
- grad_input: bfloat16 [8192, 4096], P('ctx', 'head')
- grad_b: bfloat16 [8192, 256], P(('ctx', 'head'))
- grad_c: bfloat16 [8192, 256], P(('ctx', 'head'))
Inputs may be any that keep to these rules, and one draw needn't show every extreme that they name: `doc_lengths`: they sum to 8192, and the longest document has exactly 512 tokens.
All inputs are finite; a program needn't handle non-finite values.
Results may differ from a plain program's by a relative error of at most 0.0065.
Values may be sent and summed in bfloat16 or wider, within the bound.
A program may use at most 320 MiB of HBM per device.

v0:
```python
import math

import jax
import jax.numpy as jnp
from jax import lax
from jax.sharding import PartitionSpec as P

D_HEAD = 128
PREV = 4


HIGH = lax.Precision.HIGHEST
FLOAT = jnp.float32


def shifted(value, axis, steps):
    count = lax.axis_size(axis)
    first, last = (max(0, -steps), min(count, count - steps))
    return lax.ppermute(value, axis, [(source, source + steps) for source in range(first, last)])


def carried_in_2(part, axis, combine, identity, reverse):
    count = lax.axis_size(axis)
    place = lax.axis_index(axis)
    ahead = count - 1 - place if reverse else place
    gathered = jax.tree.map(lambda a: lax.all_gather(a, axis), part)
    state = jax.tree.map(lambda a, e: jnp.zeros_like(a) + jnp.asarray(e, a.dtype), part, identity)

    def one(turn, state):
        source = count - 1 - turn if reverse else turn
        return combine(
            state, jax.tree.map(lambda a: lax.dynamic_index_in_dim(a, source, 0, False), gathered)
        )

    return lax.fori_loop(0, ahead, one, state)


def document_of(positions, lengths):
    ends = jnp.cumsum(lengths)
    return jnp.sum((positions[:, None] >= ends[None, :]).astype(jnp.int32), axis=1)


def attention_grads(query_in, key_in, value_in, grad_out, query_pos, key_pos, lengths, head_size):
    query_count = query_in.shape[0]
    key_count = key_in.shape[0]
    groups = key_in.shape[1] // head_size
    ratio = query_in.shape[1] // key_in.shape[1]
    score_scale = 1.0 / math.sqrt(head_size)
    query_doc = document_of(query_pos, lengths)
    key_doc = document_of(key_pos, lengths)
    allowed = (
        (query_doc[:, None] == key_doc[None, :])
        & (key_pos[None, :] <= query_pos[:, None])
        & (key_pos[None, :] >= 0)
    )
    query_grp = query_in.reshape(query_count, groups, ratio, head_size).transpose(1, 0, 2, 3)
    grad_grp = grad_out.reshape(query_count, groups, ratio, head_size).transpose(1, 0, 2, 3)
    key_grp = key_in.reshape(key_count, groups, head_size).transpose(1, 0, 2)
    value_grp = value_in.reshape(key_count, groups, head_size).transpose(1, 0, 2)

    def one_group(operands):
        query_h, key_h, value_h, grad_h = operands
        scores = (
            jnp.einsum("qre,ke->rqk", query_h, key_h, preferred_element_type=FLOAT) * score_scale
        )
        scores = jnp.where(allowed[None], scores, -1e30)
        row_peak = jnp.max(scores, axis=2, keepdims=True)
        weights = jnp.exp(scores - row_peak)
        normed = weights / jnp.sum(weights, axis=2, keepdims=True)
        dprobs = jnp.einsum("qre,ke->rqk", grad_h, value_h, preferred_element_type=FLOAT)
        centre = jnp.sum(normed * dprobs, axis=2, keepdims=True)
        dscores = normed * (dprobs - centre)
        dscores_low = dscores.astype(jnp.bfloat16)
        probs_low = normed.astype(jnp.bfloat16)
        grad_query = (
            jnp.einsum("rqk,ke->qre", dscores_low, key_h, preferred_element_type=FLOAT)
            * score_scale
        )
        grad_key = (
            jnp.einsum("rqk,qre->ke", dscores_low, query_h, preferred_element_type=FLOAT)
            * score_scale
        )
        grad_value = jnp.einsum("rqk,qre->ke", probs_low, grad_h, preferred_element_type=FLOAT)
        return (grad_query, grad_key, grad_value)

    grad_query, grad_key, grad_value = lax.map(one_group, (query_grp, key_grp, value_grp, grad_grp))
    grad_query = grad_query.transpose(1, 0, 2, 3).reshape(query_count, groups * ratio * head_size)
    grad_key = grad_key.transpose(1, 0, 2).reshape(key_count, groups * head_size)
    grad_value = grad_value.transpose(1, 0, 2).reshape(key_count, groups * head_size)
    return (grad_query, grad_key, grad_value)


def ssd_block(
    input_low, outgrad_low, inputs_x, outgrad, b_rows, c_rows, decay_log, token_doc, doc_before
):
    cumul = jnp.cumsum(decay_log, axis=1)
    length = token_doc.shape[0]
    order = jnp.arange(length, dtype=jnp.int32)
    causal = (order[:, None] >= order[None, :]) & (token_doc[:, None] == token_doc[None, :])
    differ = cumul[:, :, None] - cumul[:, None, :]
    within = jnp.where(causal[None], jnp.exp(jnp.where(causal[None], differ, 0.0)), 0.0)
    pairs = jnp.einsum("thp,shp->hts", outgrad_low, input_low, preferred_element_type=FLOAT)
    mixed = within * pairs
    carried_in = jnp.exp(cumul) * (token_doc == doc_before).astype(jnp.float32)[None, :]
    last_doc = token_doc[length - 1]
    to_end = (
        jnp.exp(cumul[:, length - 1 :] - cumul)
        * (token_doc == last_doc).astype(jnp.float32)[None, :]
    )
    through = jnp.exp(cumul[:, length - 1]) * (last_doc == doc_before).astype(jnp.float32)
    scaled_input = inputs_x * jnp.transpose(to_end)[:, :, None]
    scaled_grad = outgrad * jnp.transpose(carried_in)[:, :, None]
    state_local = jnp.einsum("sn,shp->hnp", b_rows, scaled_input, precision=HIGH)
    adjoint_local = jnp.einsum("sn,shp->hnp", c_rows, scaled_grad, precision=HIGH)
    return (
        within,
        mixed,
        carried_in,
        to_end,
        through,
        state_local,
        adjoint_local,
        scaled_input,
        scaled_grad,
    )


def compose(earlier, later):
    return (earlier[0] * later[0], later[0][:, None, None] * earlier[1] + later[1])


def on_device(
    queries,
    keys,
    values,
    grad_attn,
    ssm_input,
    ssm_b,
    ssm_c,
    log_decay,
    skip_gain,
    grad_ssm,
    doc_lengths,
):
    device = lax.axis_index("ctx")
    block = keys.shape[0]
    positions = device * block + jnp.arange(block, dtype=jnp.int32)
    own_pair = (keys, values)
    received = []
    for distance in range(1, PREV + 1):
        received.append(shifted((own_pair[0], own_pair[1]), "ctx", distance))
    key_rows = jnp.concatenate([pair[0] for pair in received[::-1]] + [keys], axis=0)
    value_rows = jnp.concatenate([pair[1] for pair in received[::-1]] + [values], axis=0)
    key_pos = device * block - PREV * block + jnp.arange((PREV + 1) * block, dtype=jnp.int32)
    grad_query, grad_key, grad_value = attention_grads(
        queries, key_rows, value_rows, grad_attn, positions, key_pos, doc_lengths, D_HEAD
    )

    def piece_of(array, distance):
        first = (PREV - distance) * block
        return array[first : first + block]

    total_key = piece_of(grad_key, 0)
    total_value = piece_of(grad_value, 0)
    for distance in range(1, PREV + 1):
        back_key, back_value = shifted(
            (piece_of(grad_key, distance), piece_of(grad_value, distance)), "ctx", -distance
        )
        total_key = total_key + back_key
        total_value = total_value + back_value
    mheads = log_decay.shape[0]
    head_width = ssm_input.shape[1] // mheads
    input_low = ssm_input.reshape(block, mheads, head_width)
    outgrad_low = grad_ssm.reshape(block, mheads, head_width)
    inputs_x = input_low.astype(jnp.float32)
    outgrad = outgrad_low.astype(jnp.float32)
    b_rows = ssm_b.astype(jnp.float32)
    c_rows = ssm_c.astype(jnp.float32)
    token_doc = document_of(positions, doc_lengths)
    before = document_of(positions[:1] - 1, doc_lengths)[0]
    doc_before = jnp.where(device > 0, before, -1)
    (
        within,
        mixed,
        carried_in,
        to_end,
        through,
        state_local,
        adjoint_local,
        scaled_input,
        scaled_grad,
    ) = ssd_block(
        input_low, outgrad_low, inputs_x, outgrad, b_rows, c_rows, log_decay, token_doc, doc_before
    )
    identity = (jnp.ones((mheads,), jnp.float32), jnp.zeros_like(state_local))
    state_in = carried_in_2((through, state_local), "ctx", compose, identity, False)[1]
    adjoint_in = carried_in_2((through, adjoint_local), "ctx", compose, identity, True)[1]
    grad_cc = jnp.einsum("hts,sn->tn", mixed, b_rows, precision=HIGH) + jnp.einsum(
        "thp,hnp->tn", scaled_grad, state_in, precision=HIGH
    )
    couple = jnp.dot(ssm_b, ssm_c.T, preferred_element_type=FLOAT)
    back_mix = jnp.transpose(within, (0, 2, 1)) * couple[None]
    grad_x = (
        jnp.einsum("hts,shp->thp", back_mix, outgrad, precision=HIGH)
        + jnp.einsum("tn,hnp->thp", b_rows, adjoint_in, precision=HIGH)
        * jnp.transpose(to_end)[:, :, None]
        + skip_gain[None, :, None] * outgrad
    )
    grad_bb = jnp.einsum("hst,sn->tn", mixed, c_rows, precision=HIGH) + jnp.einsum(
        "thp,hnp->tn", scaled_input, adjoint_in, precision=HIGH
    )
    summed_b, summed_c = (
        lax.psum_scatter(grad_bb, "head", scatter_dimension=0, tiled=True),
        lax.psum_scatter(grad_cc, "head", scatter_dimension=0, tiled=True),
    )
    return (
        grad_query.astype(jnp.bfloat16),
        total_key.astype(jnp.bfloat16),
        total_value.astype(jnp.bfloat16),
        grad_x.reshape(block, mheads * head_width).astype(jnp.bfloat16),
        summed_b.astype(jnp.bfloat16),
        summed_c.astype(jnp.bfloat16),
    )


def solution(mesh):
    placed = (
        P("ctx", "head"),
        P("ctx", "head"),
        P("ctx", "head"),
        P("ctx", "head"),
        P("ctx", "head"),
        P("ctx", None),
        P("ctx", None),
        P("head", "ctx"),
        P("head"),
        P("ctx", "head"),
        P(),
    )
    return jax.shard_map(
        on_device,
        mesh=mesh,
        in_specs=placed,
        out_specs=(
            P("ctx", "head"),
            P("ctx", "head"),
            P("ctx", "head"),
            P("ctx", "head"),
            P(("ctx", "head"), None),
            P(("ctx", "head"), None),
        ),
        check_vma=False,
    )
```

profile of v0, /device:TPU:1, one launch (start us, length us, event | category | flops | bytes accessed | tf_op | source)
XLA Modules:
  0.0 923.0 jit_solution(13685144731291003739)
XLA Ops:
  18.3 5.7 collective-permute-start
  24.0 6.9 collective-permute-start.1
  40.7 126.6 %all-reduce = f32[1024]{0:T(1024)S(1)} all-reduce(f32[1024]{0:T(1024)S(1)} %dynamic-update-slice), channel_id=2, replica_groups=mesh['ctx'=64,'head'=4] {'ctx'}, use_global_device_ids=true, to_apply=%add | all-reduce | flops 1024 | bytes 8192
  181.5 12.0 %while.43 = (s32[]{:T(128)}, bf16[2,128,4,128]{1,3,2,0:T(8,128)(2,1)}, f32[2,640,128]{2,1,0:T(8,128)S(1)}, f32[2,640,128]{2,1,0:T(8,128)}, bf16[2,640,128]{1,2,0...) while((s32[]{:T(128)}, ...), condition=%wide.region_7.8_spmd.clone, body=%wide.region_3.7_spmd.clone.sunk | while | flops 509035776 | bytes 18359164 | solution.py:86
  202.7 5.8 collective-permute-done.11
  209.8 6.3 collective-permute-done.10
  220.0 9.0 collective-permute-done.15
  229.0 13.7 %collective-permute-done.14 = f32[128,256]{1,0:T(8,128)S(1)} collective-permute-done((f32[128,256]{1,0:T(8,128)S(1)}, f32[128,256]{1,0:T(8,128)S(1)}, u32[]{:S(2)}, u32[]{:S(2)}) %collective-permute-start.14) | collective-permute-done | bytes 131104 | tf_op jit(solution)/shard_map/ppermute | solution.py:19
  243.4 36.0 %all-gather.6.cloned.1.call-done = f32[1024,256,64]{1,2,0:T(8,128)} async-done(((f32[16,256,64]{1,2,0:T(8,128)}), f32[1024,256,64]{1,2,0:T(8,128)}) %all-gather.6.cloned.1.call-update) | async-done | bytes 67108880 | tf_op jit(solution)/shard_map/all_gather | solution.py:26
  281.0 366.7 %while.41 = (s32[]{:T(128)}, f32[16,256,64]{2,1,0:T(8,128)}, s32[]{:T(128)}, f32[64,16]{1,0:T(8,128)}, f32[64,16,256,64]{2,3,1,0:T(8,128)}, /*index=5*/s32[]{:T(128)}, s32[]{:T(128)}, s32[]{:T(128)}, s32[]{:T(128)}) while((s32[]{:T(128)}, f32[16,256,64]{2,1,0:T(8,128)}, s32[]{:T(128)}, f32[64,16]{1,0:T(8,128)}, ...), condition=%wide.region_11.12_spmd, body=%wide.region_10.11_spmd.sunk | while | flops 524294 | bytes 7340379 | solution.py:35
  301.3 3.5 bitcast_add_fusion.6
  307.4 3.3 bitcast_add_fusion.6
  354.4 3.8 bitcast_add_fusion.6
  373.3 3.3 bitcast_add_fusion.6
  414.7 3.7 bitcast_add_fusion.6
  427.1 3.3 bitcast_add_fusion.6
  438.9 3.3 bitcast_add_fusion.6
  450.7 3.4 bitcast_add_fusion.6
  503.8 3.3 bitcast_add_fusion.6
  647.7 3.6 convolution_bitcast_fusion.8
  653.8 5.9 while.42
  659.7 3.6 convolution_bitcast_fusion.7
  668.3 4.9 reduce-scatter.3.cloned.1.call-done
  674.6 240.5 %reduce-scatter.5.cloned.1.call-done = f32[32,256]{1,0:T(8,128)} async-done(((f32[128,256]{1,0:T(8,128)}), f32[32,256]{1,0:T(8,128)}) %reduce-scatter.5.cloned.1.call-update) | async-done | bytes 32784 | tf_op jit(solution)/shard_map/reduce_scatter | solution.py:214
  (407 shorter events, 411.8 us)
Async XLA Ops:
  7.2 272.2 %all-gather.6.cloned.1.call-start = ((), (), s32[]{:S(2)}) async-start(), calls=%async_computation.4 | async-start | bytes 68157440 | tf_op jit(solution)/shard_map/all_gather | solution.py:26
  13.5 155.2 %copy-start.14 = (f32[16,128]{1,0:T(8,128)}, f32[16,128]{1,0:T(8,128)S(1)}, u32[]{:S(2)}) copy-start(f32[16,128]{1,0:T(8,128)S(1)} %reduce_window_sum.21) | copy-start | bytes 24580
  16.2 23.0 %copy-start.21 = (u32[256]{0:T(256)S(1)}, u32[256]{0:T(256)}, u32[]{:S(2)}) copy-start(u32[256]{0:T(256)} %constant.111) | copy-start | bytes 3076
  16.2 636.0 %all-gather.8.cloned.1.call-start = ((), (), s32[]{:S(2)}) async-start(), calls=%async_computation.5 | async-start | bytes 68157440 | tf_op jit(solution)/shard_map/all_gather | solution.py:26
  16.5 153.4 %copy-start.2 = (bf16[128,1024]{0,1:T(8,128)(2,1)}, bf16[128,1024]{0,1:T(8,128)(2,1)S(1)}, u32[]{:S(2)}) copy-start(bf16[128,1024]{0,1:T(8,128)(2,1)S(1)} %copy.148) | copy-start | bytes 786436
  18.1 151.9 %copy-start.6 = (bf16[128,256]{1,0:T(8,128)(2,1)S(1)}, bf16[128,256]{1,0:T(8,128)(2,1)}, u32[]{:S(2)}) copy-start(bf16[128,256]{1,0:T(8,128)(2,1)} %param.23) | copy-start | bytes 196612
  18.1 655.1 %reduce-scatter.3.cloned.1.call-start = ((), (), s32[]{:S(2)}) async-start(), calls=%async_computation.2 | async-start | bytes 163840 | tf_op jit(solution)/shard_map/reduce_scatter | solution.py:213
  18.3 152.5 %collective-permute-start = (bf16[128,256]{0,1:T(8,128)(2,1)S(1)}, bf16[128,256]{0,1:T(8,128)(2,1)S(1)}, u32[]{:S(2)}, u32[]{:S(2)}) collective-permute-start(bf16[128,256]{0,1:T(8,128)(2,1)S(1)} %copy.117), channel_id=1, source_target_pairs={{0,16},{4,20},{8,24},{12,28},{16,32},{20,36},{24,40},{28,44},{32,4... | collective-permute-start | bytes 196616 | tf_op jit(solution)/shard_map/ppermute | solution.py:19
  24.0 148.1 %collective-permute-start.1 = (bf16[128,256]{0,1:T(8,128)(2,1)S(1)}, bf16[128,256]{0,1:T(8,128)(2,1)S(1)}, u32[]{:S(2)}, u32[]{:S(2)}) collective-permute-start(bf16[128,256]{0,1:T(8,128)(2,1)S(1)} %copy.117), channel_id=1, source_target_pairs={{0,12},{4,16},{8,20},{12,24},{16,28},{20,32},{24,36},{28,40},{32,4... | collective-permute-start | bytes 196616 | tf_op jit(solution)/shard_map/ppermute | solution.py:19
  31.0 142.4 %collective-permute-start.2 = (bf16[128,256]{0,1:T(8,128)(2,1)S(1)}, bf16[128,256]{0,1:T(8,128)(2,1)S(1)}, u32[]{:S(2)}, u32[]{:S(2)}) collective-permute-start(bf16[128,256]{0,1:T(8,128)(2,1)S(1)} %copy.117), channel_id=1, source_target_pairs={{0,8},{4,12},{8,16},{12,20},{16,24},{20,28},{24,32},{28,36},{32,40... | collective-permute-start | bytes 196616 | tf_op jit(solution)/shard_map/ppermute | solution.py:19
  33.6 141.7 %collective-permute-start.3 = (bf16[128,256]{0,1:T(8,128)(2,1)S(1)}, bf16[128,256]{0,1:T(8,128)(2,1)S(1)}, u32[]{:S(2)}, u32[]{:S(2)}) collective-permute-start(bf16[128,256]{0,1:T(8,128)(2,1)S(1)} %copy.117), channel_id=1, source_target_pairs={{0,4},{4,8},{8,12},{12,16},{16,20},{20,24},{24,28},{28,32},{32,36}... | collective-permute-start | bytes 196616 | tf_op jit(solution)/shard_map/ppermute | solution.py:19
  35.7 139.8 %collective-permute-start.4 = (bf16[128,256]{0,1:T(8,128)(2,1)S(1)}, bf16[128,256]{0,1:T(8,128)(2,1)S(1)}, u32[]{:S(2)}, u32[]{:S(2)}) collective-permute-start(bf16[128,256]{0,1:T(8,128)(2,1)S(1)} %copy.123), channel_id=1, source_target_pairs={{0,16},{4,20},{8,24},{12,28},{16,32},{20,36},{24,40},{28,44},{32,4... | collective-permute-start | bytes 196616 | tf_op jit(solution)/shard_map/ppermute | solution.py:19
  170.7 5.3 collective-permute-start.5
  172.1 5.8 collective-permute-start.6
  173.4 6.8 collective-permute-start.7
  195.4 13.1 %collective-permute-start.11 = (f32[128,256]{1,0:T(8,128)S(1)}, f32[128,256]{1,0:T(8,128)S(1)}, u32[]{:S(2)}, u32[]{:S(2)}) collective-permute-start(f32[128,256]{1,0:T(8,128)S(1)} %bitcast.301), channel_id=1, source_target_pairs={{16,0},{20,4},{24,8},{28,12},{32,16},{36,20},{40,24},{44,28},{48,3... | collective-permute-start | bytes 393224 | tf_op jit(solution)/shard_map/ppermute | solution.py:19
  196.7 19.4 %collective-permute-start.10 = (f32[128,256]{1,0:T(8,128)S(1)}, f32[128,256]{1,0:T(8,128)S(1)}, u32[]{:S(2)}, u32[]{:S(2)}) collective-permute-start(f32[128,256]{1,0:T(8,128)S(1)} %bitcast.299), channel_id=1, source_target_pairs={{12,0},{16,4},{20,8},{24,12},{28,16},{32,20},{36,24},{40,28},{44,3... | collective-permute-start | bytes 393224 | tf_op jit(solution)/shard_map/ppermute | solution.py:19
  198.0 19.4 %collective-permute-start.9 = (f32[128,256]{1,0:T(8,128)S(1)}, f32[128,256]{1,0:T(8,128)S(1)}, u32[]{:S(2)}, u32[]{:S(2)}) collective-permute-start(f32[128,256]{1,0:T(8,128)S(1)} %bitcast.296), channel_id=1, source_target_pairs={{8,0},{12,4},{16,8},{20,12},{24,16},{28,20},{32,24},{36,28},{40,32... | collective-permute-start | bytes 393224 | tf_op jit(solution)/shard_map/ppermute | solution.py:19
  199.4 20.0 %collective-permute-start.8 = (f32[128,256]{1,0:T(8,128)S(1)}, f32[128,256]{1,0:T(8,128)S(1)}, u32[]{:S(2)}, u32[]{:S(2)}) collective-permute-start(f32[128,256]{1,0:T(8,128)S(1)} %bitcast.294), channel_id=1, source_target_pairs={{4,0},{8,4},{12,8},{16,12},{20,16},{24,20},{28,24},{32,28},{36,32}... | collective-permute-start | bytes 393224 | tf_op jit(solution)/shard_map/ppermute | solution.py:19
  201.4 27.6 %collective-permute-start.15 = (f32[128,256]{1,0:T(8,128)S(1)}, f32[128,256]{1,0:T(8,128)S(1)}, u32[]{:S(2)}, u32[]{:S(2)}) collective-permute-start(f32[128,256]{1,0:T(8,128)S(1)} %bitcast.297), channel_id=1, source_target_pairs={{16,0},{20,4},{24,8},{28,12},{32,16},{36,20},{40,24},{44,28},{48,3... | collective-permute-start | bytes 393224 | tf_op jit(solution)/shard_map/ppermute | solution.py:19
  208.5 34.2 %collective-permute-start.14 = (f32[128,256]{1,0:T(8,128)S(1)}, f32[128,256]{1,0:T(8,128)S(1)}, u32[]{:S(2)}, u32[]{:S(2)}) collective-permute-start(f32[128,256]{1,0:T(8,128)S(1)} %bitcast.300), channel_id=1, source_target_pairs={{12,0},{16,4},{20,8},{24,12},{28,16},{32,20},{36,24},{40,28},{44,3... | collective-permute-start | bytes 393224 | tf_op jit(solution)/shard_map/ppermute | solution.py:19
  216.1 26.6 %collective-permute-start.13 = (f32[128,256]{1,0:T(8,128)S(1)}, f32[128,256]{1,0:T(8,128)S(1)}, u32[]{:S(2)}, u32[]{:S(2)}) collective-permute-start(f32[128,256]{1,0:T(8,128)S(1)} %bitcast.298), channel_id=1, source_target_pairs={{8,0},{12,4},{16,8},{20,12},{24,16},{28,20},{32,24},{36,28},{40,32... | collective-permute-start | bytes 393224 | tf_op jit(solution)/shard_map/ppermute | solution.py:19
  217.4 25.3 %collective-permute-start.12 = (f32[128,256]{1,0:T(8,128)S(1)}, f32[128,256]{1,0:T(8,128)S(1)}, u32[]{:S(2)}, u32[]{:S(2)}) collective-permute-start(f32[128,256]{1,0:T(8,128)S(1)} %bitcast.295), channel_id=1, source_target_pairs={{4,0},{8,4},{12,8},{16,12},{20,16},{24,20},{28,24},{32,28},{36,32}... | collective-permute-start | bytes 393224 | tf_op jit(solution)/shard_map/ppermute | solution.py:19
  652.2 262.9 %reduce-scatter.5.cloned.1.call-start = ((), (), s32[]{:S(2)}) async-start(), calls=%async_computation.3 | async-start | bytes 163840 | tf_op jit(solution)/shard_map/reduce_scatter | solution.py:214
  (22 other events, 123.0 us)
Sparse Core Ops, SparseCore 0:
  16.3 263.0 all-gather.5
  282.2 241.9 all-gather.7
  652.3 20.8 reduce-scatter.2
  675.7 239.3 reduce-scatter.4
where the time goes:
time: 932 us; the launch traced here: 923 us
  waiting for transfers between devices  319 us (34%)
  other arithmetic  214 us (23%)
  local copies, waits for them, and re-layouts  184 us (20%)
  blocking collectives  127 us (14%)
  starting transfers between devices  36.6 us (4%)
  matrix products  24.8 us (3%)
  between operations  16.4 us (2%)
    reduce_scatter x1, waiting for transfers between devices, on_device(): lax.psum_scatter(grad_cc, 'head', scatter_dimension=0, tiled=True)  241 us
    add x63, other arithmetic, compose(): later[0][:, None, None] * earlier[1] + later[1]  206 us
    unnamed x1, blocking collectives  127 us
    dynamic_slice x126, local copies, waits for them, and re-layouts, one(): lax.dynamic_index_in_dim(a, source, 0, False)  122 us
    mul x63, local copies, waits for them, and re-layouts, compose(): later[0][:, None, None] * earlier[1] + later[1]  43.4 us
    ppermute x16, waiting for transfers between devices, shifted(): lax.ppermute(value, axis, [(source, source + steps) for source in range(f...  37.7 us
    ppermute x16, starting transfers between devices, shifted(): lax.ppermute(value, axis, [(source, source + steps) for source in range(f...  36.4 us
    all_gather x2, waiting for transfers between devices, carried_in_2(): gathered = jax.tree.map(lambda a: lax.all_gather(a, axis), part)  36.1 us
  transfers between devices with their start and end apart: 20, of which 9 were waited for; matrix products, arithmetic and copies ran while one was open for 44% of the time, Pallas kernels for 0%

commit v1 on v0

v1 whole, which is shorter than its diff:
```python
import math

import jax
import jax.numpy as jnp
from jax import lax
from jax.experimental import pallas as pl
from jax.experimental.pallas import tpu as pltpu
from jax.sharding import PartitionSpec as P

D_HEAD = 128
MDIM = 64
REACH = 4
SLOTS = REACH + 2

F32 = jnp.float32
BF16 = jnp.bfloat16
MESH = pl.DeviceIdType.MESH
HIGH = lax.Precision.HIGHEST


def dot(a, b, over, precision=None):
    return lax.dot_general(
        a, b, ((over[:1], over[1:]), ((), ())), precision=precision, preferred_element_type=F32
    )


def iota(shape, dim):
    return lax.broadcasted_iota(jnp.int32, shape, dim)


def document_starts(lens, base, tok):
    docs = lens.shape[1]
    row, col = iota((docs, docs), 0), iota((docs, docs), 1)
    lens_row = jnp.broadcast_to(lens.astype(F32), (docs, docs))
    lens_col = jnp.sum(jnp.where(row == col, lens_row, 0.0), axis=1, keepdims=True)
    ends_col = jnp.sum(jnp.where(col <= row, lens_row, 0.0), axis=1, keepdims=True)
    ends_row = jnp.sum(jnp.where(row <= col, lens_col, 0.0), axis=0, keepdims=True)
    at_col = (base + iota((tok, docs), 0)).astype(F32)
    at_row = (base + iota((docs, tok), 1)).astype(F32)
    start_col = jnp.max(jnp.where(at_col >= ends_row, ends_row, 0.0), axis=1, keepdims=True)
    start_row = jnp.max(jnp.where(at_row >= ends_col, ends_col, 0.0), axis=0, keepdims=True)
    return start_col, start_row


def kernel(
    shards,
    ways,
    q_ref,
    k_ref,
    v_ref,
    do_ref,
    x_ref,
    b_ref,
    c_ref,
    decay_ref,
    skip_ref,
    g_ref,
    lens_ref,
    dq_ref,
    dk_ref,
    dv_ref,
    dx_ref,
    db_ref,
    dc_ref,
    kv,
    fx,
    bg,
    fth,
    bth,
    dkv,
    mate_out,
    mate_in,
    far_out,
    far_in,
    near_out,
    near_in,
    probs,
    dscores,
    to_end,
    dx_acc,
    grads,
    y_out,
    y_in,
    send,
    recv,
):
    tok, heads = q_ref.shape[0], decay_ref.shape[0]
    kw = k_ref.shape[1]
    groups = kw // D_HEAD
    ratio = q_ref.shape[1] // kw
    width = x_ref.shape[1]
    state = b_ref.shape[1]
    shard = lax.axis_index("ctx")
    way = lax.axis_index("head")
    core = lax.rem(shard, 2)
    mate = (shard + 1 - 2 * core, way)
    up = (lax.rem(shard + 2, shards), way)
    down = (lax.rem(shard + shards - 2, shards), way)
    others = [(shard, lax.rem(way + j, ways)) for j in range(1, ways)]

    barrier = pltpu.get_barrier_semaphore()
    for peer in [mate, up, down] + others:
        pl.semaphore_signal(barrier, inc=1, device_id=peer, device_id_type=MESH)

    def rows(slot, size=tok):
        return pl.ds(pl.multiple_of(slot * size, size), size)

    def copy(ref, source, target, peer, number):
        return pltpu.make_async_remote_copy(
            src_ref=ref if source is None else ref.at[source],
            dst_ref=target,
            send_sem=send.at[number],
            recv_sem=recv.at[number],
            device_id=peer,
            device_id_type=MESH,
        )

    started = []

    def put(ref, source, target, peer, number):
        one = copy(ref, source, target, peer, number)
        one.start()
        started.append(one)

    def arrived(ref, source, number):
        copy(ref, source, ref.at[source], mate, number).wait_recv()

    class Halo:
        def __init__(self, ref, size, upward, first):
            self.ref, self.size, self.first = ref, size, first
            self.own, self.near, self.far = (4, 2, 0) if upward else (0, 2, 4)
            self.peer = up if upward else down

        def at(self, slot):
            return rows(slot, self.size)

        def send(self, slot, peer, number, target=None):
            place = self.at(slot if target is None else target)
            put(self.ref, self.at(slot), self.ref.at[place], peer, self.first + number)

        def begin(self):
            self.send(self.own + core, self.peer, 1, self.near + core)

        def begin_mate(self):
            self.send(self.own + core, mate, 0)

        def relay(self):
            arrived(self.ref, self.at(self.near + core), self.first + 1)
            self.send(self.near + core, self.peer, 3, self.far + core)
            self.send(self.near + core, mate, 2)

        def finish(self):
            arrived(self.ref, self.at(self.far + core), self.first + 3)
            self.send(self.far + core, mate, 4)

        def wait(self):
            for number, slot in ((0, self.own), (2, self.near), (4, self.far)):
                arrived(self.ref, self.at(slot + 1 - core), self.first + number)

    kv_halo = Halo(kv, tok, True, 0)
    x_halo = Halo(fx, tok, True, 5)
    g_halo = Halo(bg, tok, False, 10)
    fth_halo = Halo(fth, 8, True, 15)
    bth_halo = Halo(bth, 8, False, 20)

    own = rows(4 + core)
    kv[own, 0:kw] = k_ref[...]
    kv[own, kw : 2 * kw] = v_ref[...]
    base = shard * tok
    start_col, start_row = document_starts(lens_ref[...], base, tok)
    decay = decay_ref[...]
    later = (iota((tok, tok), 0) >= iota((tok, tok), 1)).astype(F32)
    cum_col = dot(later, decay, (1, 1), HIGH)
    cum_row = dot(decay, later, (1, 1), HIGH)
    total = cum_col[tok - 1 : tok, :]
    base_f = base.astype(F32)
    last_start = start_col[tok - 1 : tok, :]
    ending = jnp.exp(total - cum_col) * (start_col == last_start).astype(F32)
    carried = jnp.exp(cum_col) * (start_col < base_f).astype(F32)
    through = jnp.exp(total) * (last_start < base_f).astype(F32)
    table = jnp.concatenate(
        [ending, carried, jnp.broadcast_to(through, (8, heads)), jnp.broadcast_to(skip_ref[...], (8, heads))],
        axis=0,
    )
    spread = (iota((heads, width), 1) // MDIM == iota((heads, width), 0)).astype(BF16)
    table_hi = table.astype(BF16)
    table_mid = (table - table_hi.astype(F32)).astype(BF16)
    table_lo = (table - table_hi.astype(F32) - table_mid.astype(F32)).astype(BF16)
    wide = dot(table_hi, spread, (1, 0)) + dot(table_mid, spread, (1, 0)) + dot(table_lo, spread, (1, 0))
    to_end[...] = wide[0:tok]
    fx[own, 0:width] = (x_ref[...].astype(F32) * wide[0:tok]).astype(BF16)
    fx[own, width : width + state] = b_ref[...]
    g_own = rows(core)
    bg[g_own, 0:width] = (g_ref[...].astype(F32) * wide[tok : 2 * tok]).astype(BF16)
    bg[g_own, width : width + state] = c_ref[...]
    th = jnp.concatenate(
        [wide[2 * tok : 2 * tok + 1, i * (width // 8) : (i + 1) * (width // 8)] for i in range(8)], axis=0
    )
    fth[rows(4 + core, 8)] = th
    bth[rows(core, 8)] = th
    skip = wide[2 * tok + 8 : 2 * tok + 9]

    pl.semaphore_wait(barrier, 3 + len(others))
    kv_halo.begin()
    g_halo.begin()
    fth_halo.begin()
    bth_halo.begin()
    kv_halo.begin_mate()
    fth_halo.begin_mate()
    bth_halo.begin_mate()
    g_halo.begin_mate()
    x_halo.begin_mate()

    causal = (iota((tok, tok), 0) >= iota((tok, tok), 1)) & (
        start_col <= (base + iota((tok, tok), 1)).astype(F32)
    )
    couple = dot(c_ref[...], b_ref[...], (1, 1))
    low = iota((tok, 2 * MDIM), 1) < MDIM

    def pair_of_heads(pair, mix):
        part = slice(pair * 2 * MDIM, (pair + 1) * 2 * MDIM)
        grad = g_ref[:, part]
        none = jnp.zeros_like(grad)
        both = jnp.concatenate([jnp.where(low, grad, none), jnp.where(low, none, grad)], axis=0)
        pairs = dot(both, x_ref[:, part], (1, 1))
        within = [
            jnp.exp(jnp.where(causal, cum_col[:, h : h + 1] - cum_row[h : h + 1, :], -1e30))
            for h in (2 * pair, 2 * pair + 1)
        ]
        back = jnp.concatenate([w * couple for w in within], axis=0).astype(BF16)
        dx_acc[:, part] = dot(back, both, (0, 0))
        return mix + pairs[0:tok] * within[0] + pairs[tok : 2 * tok] * within[1]

    mix = jnp.zeros((tok, tok), F32)
    for pair in range(heads // 4):
        mix = pair_of_heads(pair, mix)
    kv_halo.relay()
    x_halo.begin()
    for pair in range(heads // 4, heads // 2):
        mix = pair_of_heads(pair, mix)
    mix = mix.astype(BF16)
    grad_c = dot(mix, b_ref[...], (1, 0))
    grad_b = dot(mix, c_ref[...], (0, 0))
    fth_halo.relay()
    bth_halo.relay()
    kv_halo.finish()
    g_halo.relay()
    fth_halo.finish()
    bth_halo.finish()

    kv_halo.wait()
    window = (REACH + 1) * tok
    seen = pl.ds(pl.multiple_of(core * tok, tok), window)
    key_at = (base - REACH * tok + iota((window, tok), 0)).astype(F32)
    query_at = (base + iota((window, tok), 1)).astype(F32)
    allowed = (key_at <= query_at) & (key_at >= start_row)
    bias = jnp.where(allowed, 0.0, -1e30)
    bias = jnp.concatenate([bias, bias], axis=1)
    scale = 1.0 / math.sqrt(D_HEAD)
    idle = rows(5 * (1 - core))
    dkv[idle, :] = jnp.zeros((tok, 2 * kw), F32)

    def attend(group):
        keys = kv[seen, group * D_HEAD : (group + 1) * D_HEAD]
        values = kv[seen, kw + group * D_HEAD : kw + (group + 1) * D_HEAD]
        heads_of = [slice((group * ratio + r) * D_HEAD, (group * ratio + r + 1) * D_HEAD) for r in range(ratio)]
        queries = jnp.concatenate([q_ref[:, part] for part in heads_of], axis=0)
        outgrad = jnp.concatenate([do_ref[:, part] for part in heads_of], axis=0)
        for half in range(ratio // 2):
            part = slice(half * 2 * tok, (half + 1) * 2 * tok)
            scores = dot(keys, queries[part], (1, 1)) * scale + bias
            weights = jnp.exp(scores - jnp.max(scores, axis=0, keepdims=True))
            normed = weights * (1.0 / jnp.sum(weights, axis=0, keepdims=True))
            dprobs = dot(values, outgrad[part], (1, 1))
            centre = jnp.sum(normed * dprobs, axis=0, keepdims=True)
            probs[:, part] = normed.astype(BF16)
            dscores[:, part] = (normed * (dprobs - centre)).astype(BF16)
        dkv[seen, group * D_HEAD : (group + 1) * D_HEAD] = dot(dscores[...], queries, (1, 0)) * scale
        dkv[seen, kw + group * D_HEAD : kw + (group + 1) * D_HEAD] = dot(probs[...], outgrad, (1, 0))
        grad_query = dot(dscores[...], keys, (0, 0)) * scale
        for r, part in enumerate(heads_of):
            dq_ref[:, part] = grad_query[r * tok : (r + 1) * tok].astype(BF16)

    for group in range(groups):
        attend(group)
        if group == 0:
            x_halo.relay()

    for i in range(3):
        mate_out[rows(i)] = dkv[rows(2 * i + 1 - core)].astype(BF16)
    put(mate_out, None, mate_in, mate, 25)
    g_halo.finish()
    copy(mate_out, None, mate_in, mate, 25).wait_recv()
    far_out[...] = (dkv[rows(core)] + mate_in[rows(0)].astype(F32)).astype(BF16)
    put(far_out, None, far_in, down, 26)

    def carried_state(ref, ths, step):
        first = 4 + core if step < 0 else core
        value = None
        for k in range(REACH, 0, -1):
            place = first + step * k
            block = dot(ref[rows(place), width : width + state], ref[rows(place), 0:width], (0, 0))
            if value is None:
                value = block
            else:
                th = ths[rows(place, 8)]
                th = jnp.concatenate([th[i : i + 1] for i in range(8)], axis=1)
                value = block + th * value
        return value.astype(BF16)

    g_halo.wait()
    bth_halo.wait()
    fth_halo.wait()
    adjoint = carried_state(bg, bth, 1)
    grad_b = grad_b + dot(fx[own, 0:width], adjoint, (1, 1))
    dx = dx_acc[...] + dot(b_ref[...], adjoint, (1, 0)) * to_end[...] + skip * g_ref[...].astype(F32)
    dx_ref[...] = dx.astype(BF16)

    copy(far_out, None, far_in, down, 26).wait_recv()
    near = dkv[rows(2 + core)] + mate_in[rows(1)].astype(F32) + far_in[...].astype(F32)
    near_out[...] = near.astype(BF16)
    put(near_out, None, near_in, down, 27)

    x_halo.finish()
    x_halo.wait()
    grad_c = grad_c + dot(bg[g_own, 0:width], carried_state(fx, fth, -1), (1, 1))

    share = tok // ways
    grads[0:tok] = grad_b
    grads[tok : 2 * tok] = grad_c
    for j in range(ways):
        y_out[j, 0:share] = grad_b[j * share : (j + 1) * share].astype(BF16)
        y_out[j, share : 2 * share] = grad_c[j * share : (j + 1) * share].astype(BF16)
    for j, peer in enumerate(others):
        put(y_out, peer[1], y_in.at[j], peer, 28 + j)

    copy(near_out, None, near_in, down, 27).wait_recv()
    total_kv = dkv[rows(4 + core)] + mate_in[rows(2)].astype(F32) + near_in[...].astype(F32)
    dk_ref[...] = total_kv[:, 0:kw].astype(BF16)
    dv_ref[...] = total_kv[:, kw : 2 * kw].astype(BF16)

    mine = pl.multiple_of(way * share, share)
    sum_b = grads[pl.ds(mine, share)]
    sum_c = grads[pl.ds(tok + mine, share)]
    for j in range(ways - 1):
        arrived(y_in, j, 28 + j)
        sum_b = sum_b + y_in[j, 0:share].astype(F32)
        sum_c = sum_c + y_in[j, share : 2 * share].astype(F32)
    db_ref[...] = sum_b.astype(BF16)
    dc_ref[...] = sum_c.astype(BF16)
    for one in started:
        one.wait_send()


def solution(mesh):
    shards, ways = mesh.shape["ctx"], mesh.shape["head"]

    def on_device(queries, keys, values, grad_attn, ssm_input, ssm_b, ssm_c, log_decay, skip_gain, grad_ssm, doc_lengths):
        tok, kw = keys.shape
        width, state = ssm_input.shape[1], ssm_b.shape[1]
        ratio = queries.shape[1] // kw
        transfers = 28 + ways - 1
        share = tok // ways
        vmem = pl.BlockSpec(memory_space=pltpu.VMEM)
        like = lambda a: jax.ShapeDtypeStruct(a.shape, BF16)
        part = jax.ShapeDtypeStruct((share, state), BF16)
        return pl.pallas_call(
            lambda *refs: kernel(shards, ways, *refs),
            out_shape=(like(queries), like(keys), like(values), like(ssm_input), part, part),
            in_specs=[vmem] * 11,
            out_specs=(vmem,) * 6,
            scratch_shapes=[
                pltpu.VMEM((SLOTS * tok, 2 * kw), BF16),
                pltpu.VMEM((SLOTS * tok, width + state), BF16),
                pltpu.VMEM((SLOTS * tok, width + state), BF16),
                pltpu.VMEM((SLOTS * 8, width // 8), F32),
                pltpu.VMEM((SLOTS * 8, width // 8), F32),
                pltpu.VMEM((SLOTS * tok, 2 * kw), F32),
                pltpu.VMEM((3 * tok, 2 * kw), BF16),
                pltpu.VMEM((3 * tok, 2 * kw), BF16),
                pltpu.VMEM((tok, 2 * kw), BF16),
                pltpu.VMEM((tok, 2 * kw), BF16),
                pltpu.VMEM((tok, 2 * kw), BF16),
                pltpu.VMEM((tok, 2 * kw), BF16),
                pltpu.VMEM(((REACH + 1) * tok, ratio * tok), BF16),
                pltpu.VMEM(((REACH + 1) * tok, ratio * tok), BF16),
                pltpu.VMEM((tok, width), F32),
                pltpu.VMEM((tok, width), F32),
                pltpu.VMEM((2 * tok, state), F32),
                pltpu.VMEM((ways, 2 * share, state), BF16),
                pltpu.VMEM((ways - 1, 2 * share, state), BF16),
                pltpu.SemaphoreType.DMA((transfers,)),
                pltpu.SemaphoreType.DMA((transfers,)),
            ],
            compiler_params=pltpu.CompilerParams(
                collective_id=0, has_side_effects=True, vmem_limit_bytes=48 * 1024 * 1024
            ),
        )(
            queries,
            keys,
            values,
            grad_attn,
            ssm_input,
            ssm_b,
            ssm_c,
            log_decay,
            skip_gain.reshape(1, -1),
            grad_ssm,
            doc_lengths.reshape(1, -1),
        )

    both = P("ctx", "head")
    rows = P(("ctx", "head"), None)
    return jax.shard_map(
        on_device,
        mesh=mesh,
        in_specs=(both, both, both, both, both, P("ctx", None), P("ctx", None), P("head", "ctx"), P("head"), both, P()),
        out_specs=(both, both, both, both, rows, rows),
        check_vma=False,
    )
```

time: 932 us -> 55.4 us (0.06)
  waiting for transfers between devices: 319 us -> 0 us
  other arithmetic: 214 us -> 0 us
  local copies, waits for them, and re-layouts: 184 us -> 12.4 us
  blocking collectives: 127 us -> 0 us
  Pallas kernels: 0 us -> 41.9 us
  starting transfers between devices: 36.6 us -> 0 us
  matrix products: 24.8 us -> 0 us
  between operations: 16.4 us -> 0.67 us
    reduce_scatter x2 -> x0, waiting for transfers between devices: 245 us -> none  [the longest x1 241 us: on_device(): lax.psum_scatter(grad_cc, 'head', scatter_dimension=0, tiled=True)]
    add x65 -> x0, other arithmetic: 206 us -> none  [the longest x63 206 us: compose(): later[0][:, None, None] * earlier[1] + later[1]]
    unnamed x1 -> x0, blocking collectives: 127 us -> none
    dynamic_slice x126 -> x0, local copies, waits for them, and re-layouts: 122 us -> none  [one(): lax.dynamic_index_in_dim(a, source, 0, False)]
    mul x63 -> x0, local copies, waits for them, and re-layouts: 43.4 us -> none  [compose(): later[0][:, None, None] * earlier[1] + later[1]]
    pallas_call x0 -> x1, Pallas kernels: none -> 41.9 us  [on_device(): pl.pallas_call(lambda *refs: kernel(shards, ways, *refs), out_shape=(like...]
    ppermute x16 -> x0, waiting for transfers between devices: 37.7 us -> none  [shifted(): lax.ppermute(value, axis, [(source, source + steps) for source in range(f...]
    ppermute x16 -> x0, starting transfers between devices: 36.4 us -> none  [shifted(): lax.ppermute(value, axis, [(source, source + steps) for source in range(f...]
  transfers between devices with their start and end apart: 20 -> 0, of which waited for: 9 -> 0; matrix products, arithmetic and copies ran while one was open for 44% -> 0% of each run, Pallas kernels for 0% -> 0%
where the time goes in v1:
time: 55.4 us; the launch traced here: 55 us
  Pallas kernels  41.9 us (76%)
  local copies, waits for them, and re-layouts  12.4 us (22%)
  between operations  0.67 us (1%)
    pallas_call x1, Pallas kernels, on_device(): pl.pallas_call(lambda *refs: kernel(shards, ways, *refs), out_shape=(like...  41.9 us
    unnamed x28, local copies, waits for them, and re-layouts  12.4 us

profile of v1, /device:TPU:1, one launch (start us, length us, event | category | flops | bytes accessed | tf_op | source)
XLA Modules:
  0.0 55.0 jit_solution(12972885396124982865)
XLA Ops:
  0.6 0.0 copy-start.9
  0.6 0.0 copy-start.10
  0.7 0.6 %copy-done.9 = f32[16]{0:T(128)S(1)} copy-done((f32[16]{0:T(128)S(1)}, f32[16]{0:T(128)}, u32[]{:S(2)}) %copy-start.9) | copy-done | bytes 88
  1.3 0.0 copy-done.10
  1.3 0.0 copy-start
  1.3 0.9 %copy-done = bf16[128,1024]{1,0:T(8,128)(2,1)S(1)} copy-done((bf16[128,1024]{1,0:T(8,128)(2,1)S(1)}, bf16[128,1024]{1,0:T(8,128)(2,1)}, u32[]{:S(2)}) %copy-start) | copy-done | bytes 262168
  2.3 0.0 copy-start.1
  2.3 0.9 %copy-done.1 = bf16[128,1024]{1,0:T(8,128)(2,1)S(1)} copy-done((bf16[128,1024]{1,0:T(8,128)(2,1)S(1)}, bf16[128,1024]{1,0:T(8,128)(2,1)}, u32[]{:S(2)}) %copy-start.1) | copy-done | bytes 262168
  3.2 0.0 copy-start.2
  3.2 0.9 %copy-done.2 = bf16[128,1024]{1,0:T(8,128)(2,1)S(1)} copy-done((bf16[128,1024]{1,0:T(8,128)(2,1)S(1)}, bf16[128,1024]{1,0:T(8,128)(2,1)}, u32[]{:S(2)}) %copy-start.2) | copy-done | bytes 262168
  4.2 0.0 copy-start.3
  4.2 0.9 %copy-done.3 = bf16[128,1024]{1,0:T(8,128)(2,1)S(1)} copy-done((bf16[128,1024]{1,0:T(8,128)(2,1)S(1)}, bf16[128,1024]{1,0:T(8,128)(2,1)}, u32[]{:S(2)}) %copy-start.3) | copy-done | bytes 262168
  5.1 0.8 %copy-done.4 = bf16[128,256]{1,0:T(8,128)(2,1)S(1)} copy-done((bf16[128,256]{1,0:T(8,128)(2,1)S(1)}, bf16[128,256]{1,0:T(8,128)(2,1)}, u32[]{:S(2)}) %copy-start.4) | copy-done | bytes 65560
  6.0 0.8 %copy-done.5 = bf16[128,256]{1,0:T(8,128)(2,1)S(1)} copy-done((bf16[128,256]{1,0:T(8,128)(2,1)S(1)}, bf16[128,256]{1,0:T(8,128)(2,1)}, u32[]{:S(2)}) %copy-start.5) | copy-done | bytes 65560
  6.8 0.8 %copy-done.6 = bf16[128,256]{1,0:T(8,128)(2,1)S(1)} copy-done((bf16[128,256]{1,0:T(8,128)(2,1)S(1)}, bf16[128,256]{1,0:T(8,128)(2,1)}, u32[]{:S(2)}) %copy-start.6) | copy-done | bytes 65560
  7.6 0.8 %copy-done.7 = bf16[128,256]{1,0:T(8,128)(2,1)S(1)} copy-done((bf16[128,256]{1,0:T(8,128)(2,1)S(1)}, bf16[128,256]{1,0:T(8,128)(2,1)}, u32[]{:S(2)}) %copy-start.7) | copy-done | bytes 65560
  8.5 0.7 %copy-done.8 = f32[16,128]{1,0:T(8,128)S(1)} copy-done((f32[16,128]{1,0:T(8,128)S(1)}, f32[16,128]{1,0:T(8,128)}, u32[]{:S(2)}) %copy-start.8) | copy-done | bytes 8216
  9.2 41.9 %shard_map.154 = (bf16[128,1024]{1,0:T(8,128)(2,1)S(1)}, bf16[128,256]{1,0:T(8,128)(2,1)S(1)}, bf16[128,256]{1,0:T(8,128)(2,1)S(1)}, bf16[128,1024]{1,0:T(8,128)...) custom-call(bf16[128,1024]{1,0:T(8,128)(2,1)S(1)} %copy-done, bf16[128,256]{1,0:T(8,128)(2,1)S(1)} %copy-done.4, ...), custom_call_target="tpu_custom_call" | custom-call | tf_op jit(solution)/shard_map/pallas_call | solution.py:367
  51.1 0.7 %copy.23 = bf16[128,1024]{1,0:T(8,128)(2,1)} copy(bf16[128,1024]{1,0:T(8,128)(2,1)S(1)} %get-tuple-element.12) | data formatting | bytes 524288
  51.8 0.6 %copy.24 = bf16[128,256]{1,0:T(8,128)(2,1)} copy(bf16[128,256]{1,0:T(8,128)(2,1)S(1)} %get-tuple-element.13) | data formatting | bytes 131072
  52.4 0.6 %copy.25 = bf16[128,256]{1,0:T(8,128)(2,1)} copy(bf16[128,256]{1,0:T(8,128)(2,1)S(1)} %get-tuple-element.14) | data formatting | bytes 131072
  53.0 0.7 %copy.26 = bf16[128,1024]{1,0:T(8,128)(2,1)} copy(bf16[128,1024]{1,0:T(8,128)(2,1)S(1)} %get-tuple-element.15) | data formatting | bytes 524288
  53.7 0.6 %copy.27 = bf16[32,256]{1,0:T(8,128)(2,1)} copy(bf16[32,256]{1,0:T(8,128)(2,1)S(1)} %get-tuple-element.16) | data formatting | bytes 32768
  54.3 0.6 %copy.28 = bf16[32,256]{1,0:T(8,128)(2,1)} copy(bf16[32,256]{1,0:T(8,128)(2,1)S(1)} %get-tuple-element.17) | data formatting | bytes 32768
  (5 shorter events, 0.0 us)
Async XLA Ops:
  0.6 0.7 %copy-start.9 = (f32[16]{0:T(128)S(1)}, f32[16]{0:T(128)}, u32[]{:S(2)}) copy-start(f32[16]{0:T(128)} %param.19) | copy-start | bytes 196
  0.6 0.7 %copy-start.10 = (s32[32]{0:T(128)S(1)}, s32[32]{0:T(128)}, u32[]{:S(2)}) copy-start(s32[32]{0:T(128)} %param.21) | copy-start | bytes 388
  1.3 0.9 %copy-start = (bf16[128,1024]{1,0:T(8,128)(2,1)S(1)}, bf16[128,1024]{1,0:T(8,128)(2,1)}, u32[]{:S(2)}) copy-start(bf16[128,1024]{1,0:T(8,128)(2,1)} %refs_0_.1) | copy-start | bytes 786436
  2.3 0.9 %copy-start.1 = (bf16[128,1024]{1,0:T(8,128)(2,1)S(1)}, bf16[128,1024]{1,0:T(8,128)(2,1)}, u32[]{:S(2)}) copy-start(bf16[128,1024]{1,0:T(8,128)(2,1)} %refs_3_.1) | copy-start | bytes 786436
  3.2 0.9 %copy-start.2 = (bf16[128,1024]{1,0:T(8,128)(2,1)S(1)}, bf16[128,1024]{1,0:T(8,128)(2,1)}, u32[]{:S(2)}) copy-start(bf16[128,1024]{1,0:T(8,128)(2,1)} %refs_4_.1) | copy-start | bytes 786436
  4.2 0.9 %copy-start.3 = (bf16[128,1024]{1,0:T(8,128)(2,1)S(1)}, bf16[128,1024]{1,0:T(8,128)(2,1)}, u32[]{:S(2)}) copy-start(bf16[128,1024]{1,0:T(8,128)(2,1)} %refs_9_.1) | copy-start | bytes 786436
  5.1 0.8 %copy-start.4 = (bf16[128,256]{1,0:T(8,128)(2,1)S(1)}, bf16[128,256]{1,0:T(8,128)(2,1)}, u32[]{:S(2)}) copy-start(bf16[128,256]{1,0:T(8,128)(2,1)} %refs_1_.1) | copy-start | bytes 196612
  6.0 0.8 %copy-start.5 = (bf16[128,256]{1,0:T(8,128)(2,1)S(1)}, bf16[128,256]{1,0:T(8,128)(2,1)}, u32[]{:S(2)}) copy-start(bf16[128,256]{1,0:T(8,128)(2,1)} %refs_2_.1) | copy-start | bytes 196612
  6.8 0.8 %copy-start.6 = (bf16[128,256]{1,0:T(8,128)(2,1)S(1)}, bf16[128,256]{1,0:T(8,128)(2,1)}, u32[]{:S(2)}) copy-start(bf16[128,256]{1,0:T(8,128)(2,1)} %refs_5_.1) | copy-start | bytes 196612
  7.6 0.8 %copy-start.7 = (bf16[128,256]{1,0:T(8,128)(2,1)S(1)}, bf16[128,256]{1,0:T(8,128)(2,1)}, u32[]{:S(2)}) copy-start(bf16[128,256]{1,0:T(8,128)(2,1)} %refs_6_.1) | copy-start | bytes 196612
  8.5 0.7 %copy-start.8 = (f32[16,128]{1,0:T(8,128)S(1)}, f32[16,128]{1,0:T(8,128)}, u32[]{:S(2)}) copy-start(f32[16,128]{1,0:T(8,128)} %refs_7_.1) | copy-start | bytes 24580

commit v2 on v1

v2 whole, which is shorter than its diff:
```python
import math

import jax
import jax.numpy as jnp
from jax import lax
from jax.experimental import pallas as pl
from jax.experimental.pallas import tpu as pltpu
from jax.sharding import PartitionSpec as P

D_HEAD = 128
MDIM = 64
REACH = 4
SLOTS = REACH + 2
TRANSFERS = 72
VMEM_BYTES = 56 * 1024 * 1024

F32 = jnp.float32
BF16 = jnp.bfloat16
MESH = pl.DeviceIdType.MESH
HIGH = lax.Precision.HIGHEST


def dot(a, b, over, precision=None):
    return lax.dot_general(
        a, b, ((over[:1], over[1:]), ((), ())), precision=precision, preferred_element_type=F32
    )


def iota(shape, dim):
    return lax.broadcasted_iota(jnp.int32, shape, dim)


def document_starts(lens, base, tok):
    docs = lens.shape[1]
    row, col = iota((docs, docs), 0), iota((docs, docs), 1)
    lens_row = jnp.broadcast_to(lens.astype(F32), (docs, docs))
    lens_col = jnp.sum(jnp.where(row == col, lens_row, 0.0), axis=1, keepdims=True)
    ends_col = jnp.sum(jnp.where(col <= row, lens_row, 0.0), axis=1, keepdims=True)
    ends_row = jnp.sum(jnp.where(row <= col, lens_col, 0.0), axis=0, keepdims=True)
    at_col = (base + iota((tok, docs), 0)).astype(F32)
    at_row = (base + iota((docs, tok), 1)).astype(F32)
    start_col = jnp.max(jnp.where(at_col >= ends_row, ends_row, 0.0), axis=1, keepdims=True)
    start_row = jnp.max(jnp.where(at_row >= ends_col, ends_col, 0.0), axis=0, keepdims=True)
    return start_col, start_row


def kernel(
    shards,
    ways,
    q_hbm,
    k_hbm,
    v_hbm,
    do_hbm,
    x_hbm,
    b_hbm,
    c_hbm,
    decay_hbm,
    skip_hbm,
    g_hbm,
    lens_hbm,
    dq_ref,
    dk_ref,
    dv_ref,
    dx_ref,
    db_ref,
    dc_ref,
    q_ref,
    do_ref,
    x_ref,
    b_ref,
    decay_ref,
    skip_ref,
    g_ref,
    lens_ref,
    kv,
    fx,
    fth,
    ga,
    gb,
    bc,
    bth,
    xs,
    dkv,
    mate_out,
    mate_in,
    far_out,
    far_in,
    near_out,
    near_in,
    probs,
    dscores,
    to_end,
    dx_acc,
    near_adjoint,
    early,
    early_out,
    early_in,
    late,
    late_out,
    late_in,
    last,
    last_out,
    last_in,
    ahead_out,
    ahead_in,
    send,
    recv,
    load,
    ready,
):
    tok, heads = q_ref.shape[0], decay_ref.shape[0]
    kw = k_hbm.shape[1]
    groups = kw // D_HEAD
    ratio = q_ref.shape[1] // kw
    width = x_ref.shape[1]
    share = tok // ways
    half = width // 2
    shard = lax.axis_index("ctx")
    way = lax.axis_index("head")
    core = lax.rem(shard, 2)

    def along(steps):
        return (lax.rem(shard + (steps + shards), shards), way)

    mate = (shard + 1 - 2 * core, way)
    up, down = along(2), along(-2)
    others = [(shard, lax.rem(way + j, ways)) for j in range(1, ways)]
    barrier = pltpu.get_barrier_semaphore()
    for peer in [along(-k) for k in range(1, REACH + 1)] + [mate] + others:
        pl.semaphore_signal(barrier, inc=1, device_id=peer, device_id_type=MESH)

    def rows(slot, size=tok):
        return pl.ds(pl.multiple_of(slot * size, size), size)

    numbers = {}

    def copy(source, target, peer, name):
        number = numbers.setdefault(name, len(numbers))
        return pltpu.make_async_remote_copy(
            src_ref=source,
            dst_ref=target,
            send_sem=send.at[number],
            recv_sem=recv.at[number],
            device_id=peer,
            device_id_type=MESH,
        )

    started = []

    def put(source, target, peer, name):
        one = copy(source, target, peer, name)
        one.start()
        started.append(one)

    def arrived(target, name):
        copy(target, target, mate, name).wait_recv()

    class Halo:
        def __init__(self, name, upward, view):
            self.name, self.view = name, view
            self.own, self.near, self.far = (4, 2, 0) if upward else (0, 2, 4)
            self.peer = up if upward else down

        def send(self, slot, peer, what, target=None):
            place = self.view(slot if target is None else target)
            put(self.view(slot), place, peer, (self.name, what))

        def begin(self):
            self.send(self.own + core, self.peer, "near", self.near + core)

        def begin_mate(self):
            self.send(self.own + core, mate, "mate own")

        def relay(self):
            arrived(self.view(self.near + core), (self.name, "near"))
            self.send(self.near + core, self.peer, "far", self.far + core)
            self.send(self.near + core, mate, "mate near")

        def finish(self):
            arrived(self.view(self.far + core), (self.name, "far"))
            self.send(self.far + core, mate, "mate far")

        def wait_near(self):
            arrived(self.view(self.own + 1 - core), (self.name, "mate own"))
            arrived(self.view(self.near + 1 - core), (self.name, "mate near"))

        def wait_far(self):
            arrived(self.view(self.far + 1 - core), (self.name, "mate far"))

    kv_halos = [Halo(("kv", i), True, lambda slot, i=i: kv.at[i, rows(slot)]) for i in range(groups)]
    x_halo = Halo("x", True, lambda slot: fx.at[rows(slot)])
    fth_halo = Halo("fth", True, lambda slot: fth.at[rows(slot, 8)])
    ga_halo = Halo("ga", False, lambda slot: ga.at[rows(slot)])
    gb_halo = Halo("gb", False, lambda slot: gb.at[rows(slot)])
    bth_halo = Halo("bth", False, lambda slot: bth.at[rows(slot, 8)])

    def c_part(slot, of):
        return bc.at[pl.ds(pl.multiple_of(slot * tok + of * share, share), share)]

    def c_spread(slot, name):
        for j, peer in enumerate(others):
            put(c_part(slot, way), c_part(slot, way), peer, ("c", name, j))

    def c_gather(slot, name):
        for j in range(ways - 1):
            arrived(c_part(slot, lax.rem(way + (ways - 1 - j), ways)), ("c", name, j))
        put(bc.at[rows(slot)], bc.at[rows(slot)], mate, ("c", "mate", name))

    own = rows(4 + core)
    g_own = rows(core)
    loads = {}
    places = [
        ("lens", lens_hbm, lens_ref),
        ("decay", decay_hbm, decay_ref),
        ("skip", skip_hbm, skip_ref),
    ]
    for i in range(groups):
        part_of = slice(i * D_HEAD, (i + 1) * D_HEAD)
        places.append(("k", k_hbm.at[:, part_of], kv.at[i, own, 0:D_HEAD]))
        places.append(("v", v_hbm.at[:, part_of], kv.at[i, own, D_HEAD : 2 * D_HEAD]))
    places += [
        ("c", c_hbm, bc.at[g_own]),
        ("g", g_hbm, g_ref),
        ("x", x_hbm, x_ref),
        ("b", b_hbm, b_ref),
        ("q", q_hbm, q_ref),
        ("do", do_hbm, do_ref),
    ]
    for number, (name, source, target) in enumerate(places):
        one = pltpu.make_async_copy(source, target, load.at[number])
        one.start()
        loads.setdefault(name, []).append(one)

    def loaded(*names):
        for name in names:
            for one in loads[name]:
                one.wait()

    loaded("lens", "decay", "skip")
    base = shard * tok
    start_col, start_row = document_starts(lens_ref[...], base, tok)
    decay = decay_ref[...]
    later = (iota((tok, tok), 0) >= iota((tok, tok), 1)).astype(F32)
    cum_col = dot(later, decay, (1, 1), HIGH)
    cum_row = dot(decay, later, (1, 1), HIGH)
    total = cum_col[tok - 1 : tok, :]
    base_f = base.astype(F32)
    last_start = start_col[tok - 1 : tok, :]
    ending = jnp.exp(total - cum_col) * (start_col == last_start).astype(F32)
    carried = jnp.exp(cum_col) * (start_col < base_f).astype(F32)
    through = jnp.exp(total) * (last_start < base_f).astype(F32)
    table = jnp.concatenate(
        [ending, carried, jnp.broadcast_to(through, (8, heads)), jnp.broadcast_to(skip_ref[...], (8, heads))],
        axis=0,
    )
    spread = (iota((heads, width), 1) // MDIM == iota((heads, width), 0)).astype(BF16)
    table_hi = table.astype(BF16)
    table_mid = (table - table_hi.astype(F32)).astype(BF16)
    table_lo = (table - table_hi.astype(F32) - table_mid.astype(F32)).astype(BF16)
    wide = dot(table_hi, spread, (1, 0)) + dot(table_mid, spread, (1, 0)) + dot(table_lo, spread, (1, 0))
    skip = wide[2 * tok + 8 : 2 * tok + 9]
    th = jnp.concatenate(
        [wide[2 * tok : 2 * tok + 1, i * (width // 8) : (i + 1) * (width // 8)] for i in range(8)], axis=0
    )
    bth[rows(core, 8)] = th
    fth[rows(4 + core, 8)] = th
    to_end[...] = wide[0:tok]

    loaded("k", "v")
    pl.semaphore_wait(barrier, REACH + 1 + len(others))
    pl.semaphore_signal(ready, inc=1, device_id=up, device_id_type=MESH)
    for halo in kv_halos:
        halo.begin()
    for halo in kv_halos:
        halo.begin_mate()
    loaded("g", "c")
    scaled = (g_ref[...].astype(F32) * wide[tok : 2 * tok]).astype(BF16)
    ga[g_own] = scaled[:, 0:half]
    gb[g_own] = scaled[:, half:]
    pl.semaphore_wait(ready, 1)
    put(c_part(core, way), c_part(2 + core, way), down, ("c", "near"))
    bth_halo.begin()
    ga_halo.begin()
    gb_halo.begin()
    loaded("x", "b")
    xs[...] = (x_ref[...].astype(F32) * wide[0:tok]).astype(BF16)
    fx[own, 0:half] = xs[:, half:]
    fx[own, half:] = b_ref[...]
    fth_halo.begin()
    for halo in (fth_halo, bth_halo, ga_halo, gb_halo, x_halo):
        halo.begin_mate()
    put(bc.at[g_own], bc.at[g_own], mate, ("c", "mate", "own"))
    state = dot(b_ref[...], xs[:, 0:half], (0, 0))

    causal = (iota((tok, tok), 0) >= iota((tok, tok), 1)) & (
        start_col <= (base + iota((tok, tok), 1)).astype(F32)
    )
    couple = dot(bc[g_own], b_ref[...], (1, 1))
    low = iota((tok, 2 * MDIM), 1) < MDIM

    def pair_of_heads(pair, mix):
        part = slice(pair * 2 * MDIM, (pair + 1) * 2 * MDIM)
        grad = g_ref[:, part]
        none = jnp.zeros_like(grad)
        both = jnp.concatenate([jnp.where(low, grad, none), jnp.where(low, none, grad)], axis=0)
        pairs = dot(both, x_ref[:, part], (1, 1))
        within = [
            jnp.exp(jnp.where(causal, cum_col[:, h : h + 1] - cum_row[h : h + 1, :], -1e30))
            for h in (2 * pair, 2 * pair + 1)
        ]
        back = jnp.concatenate([w * couple for w in within], axis=0).astype(BF16)
        dx_acc[:, part] = dot(back, both, (0, 0))
        return mix + pairs[0:tok] * within[0] + pairs[tok : 2 * tok] * within[1]

    mix = jnp.zeros((tok, tok), F32)
    for pair in range(heads // 4):
        mix = pair_of_heads(pair, mix)
    kv_halos[0].relay()
    for pair in range(heads // 4, heads // 2 - 2):
        mix = pair_of_heads(pair, mix)
    for halo in kv_halos[1:]:
        halo.relay()
    x_halo.begin()
    for pair in range(heads // 2 - 2, heads // 2):
        mix = pair_of_heads(pair, mix)
    mix = mix.astype(BF16)
    last[0:tok] = dot(mix, bc[g_own], (0, 0))
    last[tok : 2 * tok] = dot(mix, b_ref[...], (1, 0))
    arrived(c_part(2 + core, way), ("c", "near"))
    put(c_part(2 + core, way), c_part(4 + core, way), down, ("c", "far"))
    c_spread(2 + core, "near")
    bth_halo.relay()
    fth_halo.relay()
    kv_halos[0].finish()
    ga_halo.relay()
    kv_halos[1].finish()

    loaded("q", "do")
    window = (REACH + 1) * tok
    seen = pl.ds(pl.multiple_of(core * tok, tok), window)
    key_at = (base - REACH * tok + iota((window, tok), 0)).astype(F32)
    query_at = (base + iota((window, tok), 1)).astype(F32)
    allowed = (key_at <= query_at) & (key_at >= start_row)
    bias = jnp.where(allowed, 0.0, -1e30)
    bias = jnp.concatenate([bias, bias], axis=1)
    scale = 1.0 / math.sqrt(D_HEAD)
    idle = rows(5 * (1 - core))

    def attend(group):
        keys = kv[group, seen, 0:D_HEAD]
        values = kv[group, seen, D_HEAD : 2 * D_HEAD]
        heads_of = [slice((group * ratio + r) * D_HEAD, (group * ratio + r + 1) * D_HEAD) for r in range(ratio)]
        queries = jnp.concatenate([q_ref[:, part] for part in heads_of], axis=0)
        outgrad = jnp.concatenate([do_ref[:, part] for part in heads_of], axis=0)
        for half in range(ratio // 2):
            part = slice(half * 2 * tok, (half + 1) * 2 * tok)
            scores = dot(keys, queries[part], (1, 1)) * scale + bias
            weights = jnp.exp(scores - jnp.max(scores, axis=0, keepdims=True))
            normed = weights * (1.0 / jnp.sum(weights, axis=0, keepdims=True))
            dprobs = dot(values, outgrad[part], (1, 1))
            centre = jnp.sum(normed * dprobs, axis=0, keepdims=True)
            probs[:, part] = normed.astype(BF16)
            dscores[:, part] = (normed * (dprobs - centre)).astype(BF16)
        dkv[group, idle] = jnp.zeros((tok, 2 * D_HEAD), F32)
        dkv[group, seen, 0:D_HEAD] = dot(dscores[...], queries, (1, 0)) * scale
        dkv[group, seen, D_HEAD : 2 * D_HEAD] = dot(probs[...], outgrad, (1, 0))
        for i in range(3):
            mate_out[group, rows(i)] = dkv[group, rows(2 * i + 1 - core)].astype(BF16)
        put(mate_out.at[group], mate_in.at[group], mate, ("dkv mate", group))
        grad_query = dot(dscores[...], keys, (0, 0)) * scale
        for r, part in enumerate(heads_of):
            dq_ref[:, part] = grad_query[r * tok : (r + 1) * tok].astype(BF16)

    def send_far(group):
        arrived(mate_in.at[group], ("dkv mate", group))
        far_out[group] = (dkv[group, rows(core)] + mate_in[group, rows(0)].astype(F32)).astype(BF16)
        put(far_out.at[group], far_in.at[group], down, ("dkv far", group))

    def send_near(group):
        arrived(far_in.at[group], ("dkv far", group))
        near = dkv[group, rows(2 + core)] + mate_in[group, rows(1)].astype(F32) + far_in[group].astype(F32)
        near_out[group] = near.astype(BF16)
        put(near_out.at[group], near_in.at[group], down, ("dkv near", group))

    def finish_keys(group):
        arrived(near_in.at[group], ("dkv near", group))
        total_kv = dkv[group, rows(4 + core)] + mate_in[group, rows(2)].astype(F32) + near_in[group].astype(F32)
        part = slice(group * D_HEAD, (group + 1) * D_HEAD)
        dk_ref[:, part] = total_kv[:, 0:D_HEAD].astype(BF16)
        dv_ref[:, part] = total_kv[:, D_HEAD : 2 * D_HEAD].astype(BF16)

    for group in range(groups):
        kv_halos[group].wait_near()
        kv_halos[group].wait_far()
        attend(group)
        if group == 0:
            gb_halo.relay()
            x_halo.relay()
            arrived(c_part(4 + core, way), ("c", "far"))
            c_spread(4 + core, "far")
            c_gather(2 + core, "near")
        else:
            send_far(group - 1)

    def decay_through(ths, slot):
        row = ths[rows(slot, 8)]
        return jnp.concatenate([row[i : i + 1] for i in range(8)], axis=1)

    def adjoint_of(ref, k):
        return dot(bc[rows(core + k)], ref[rows(core + k)], (0, 0))

    def ahead(k, factor):
        value = state if factor is None else state * factor[:, 0:half]
        return dot(ga[rows(core + k)], value.astype(BF16), (1, 1))

    def finish_input(part, adjoint):
        last[0:tok] = last[0:tok] + dot(xs[:, part], adjoint, (1, 1))
        dx = dx_acc[:, part] + dot(b_ref[...], adjoint, (1, 0)) * to_end[:, part]
        dx_ref[:, part] = (dx + skip[:, part] * g_ref[:, part].astype(F32)).astype(BF16)

    def sum_start(held, out, into, name, first, last):
        span = pl.ds(first * share, (last - first) * share)
        for j in range(ways):
            for i in range(first, last):
                part = held[i * tok + j * share : i * tok + (j + 1) * share]
                out[j, i * share : (i + 1) * share] = part.astype(BF16)
        for j, peer in enumerate(others):
            put(out.at[peer[1], span], into.at[j, span], peer, (name, first, j))

    def sum_finish(held, into, name, first, last):
        span = pl.ds(first * share, (last - first) * share)
        for j in range(ways - 1):
            arrived(into.at[j, span], (name, first, j))
        values = []
        for i in range(first, last):
            value = held[pl.ds(pl.multiple_of(i * tok + way * share, share), share)]
            for j in range(ways - 1):
                value = value + into[j, i * share : (i + 1) * share].astype(F32)
            values.append(value)
        return values

    def send_ahead(k, value):
        ahead_out[k - 1] = value.astype(BF16)
        put(ahead_out.at[k - 1], ahead_in.at[k - 1], along(k), ("ahead", k))

    first_half, second_half = slice(0, half), slice(half, width)
    ga_halo.wait_near()
    bth_halo.wait_near()
    th1 = decay_through(bth, core + 1)
    early[0:tok] = ahead(1, None)
    early[tok : 2 * tok] = ahead(2, th1)
    sum_start(early, early_out, early_in, "early", 0, 2)
    send_far(groups - 1)
    ga_halo.finish()
    bth_halo.finish()
    fth_halo.finish()
    c_gather(4 + core, "far")
    arrived(bc.at[rows(1 - core)], ("c", "mate", "own"))
    arrived(bc.at[rows(3 - core)], ("c", "mate", "near"))
    near_adjoint[:, first_half] = adjoint_of(ga, 1) + th1[:, first_half] * adjoint_of(ga, 2)
    gb_halo.wait_near()
    near_adjoint[:, second_half] = adjoint_of(gb, 1) + th1[:, second_half] * adjoint_of(gb, 2)
    bth_halo.wait_far()
    th2 = th1 * decay_through(bth, core + 2)
    th3 = decay_through(bth, core + 3)
    ga_halo.wait_far()
    late[0:tok] = ahead(3, th2)
    late[tok : 2 * tok] = ahead(4, th2 * th3)
    sum_start(late, late_out, late_in, "late", 0, 2)
    ahead_1, ahead_2 = sum_finish(early, early_in, "early", 0, 2)
    send_ahead(1, ahead_1)
    send_ahead(2, ahead_2)
    for group in range(groups):
        send_near(group)
    x_halo.finish()
    arrived(bc.at[rows(5 - core)], ("c", "mate", "far"))

    def adjoint(ref, part):
        far = adjoint_of(ref, 3) + th3[:, part] * adjoint_of(ref, 4)
        return (near_adjoint[:, part] + th2[:, part] * far).astype(BF16)

    finish_input(first_half, adjoint(ga, first_half))
    ahead_3, ahead_4 = sum_finish(late, late_in, "late", 0, 2)
    send_ahead(3, ahead_3)
    send_ahead(4, ahead_4)
    gb_halo.finish()

    x_halo.wait_near()
    fth_halo.wait_near()
    fth_halo.wait_far()
    x_halo.wait_far()
    state_in = None
    for k in range(REACH, 0, -1):
        place = 4 + core - k
        value = dot(fx[rows(place), half:], fx[rows(place), 0:half], (0, 0))
        state_in = value if state_in is None else value + decay_through(fth, place)[:, half:] * state_in
    last[tok : 2 * tok] = last[tok : 2 * tok] + dot(gb[g_own], state_in.astype(BF16), (1, 1))
    sum_start(last, last_out, last_in, "last", 1, 2)
    gb_halo.wait_far()
    finish_input(second_half, adjoint(gb, second_half))
    sum_start(last, last_out, last_in, "last", 0, 1)
    for group in range(groups):
        finish_keys(group)
    (sum_c,) = sum_finish(last, last_in, "last", 1, 2)
    for k in range(1, REACH + 1):
        arrived(ahead_in.at[k - 1], ("ahead", k))
        sum_c = sum_c + ahead_in[k - 1].astype(F32)
    dc_ref[...] = sum_c.astype(BF16)
    (sum_b,) = sum_finish(last, last_in, "last", 0, 1)
    db_ref[...] = sum_b.astype(BF16)
    for one in started:
        one.wait_send()


def hand_over(*refs):
    count = len(refs) // 2
    for i in range(count):
        refs[count + i][...] = refs[i][...]


def solution(mesh):
    shards, ways = mesh.shape["ctx"], mesh.shape["head"]

    def on_device(queries, keys, values, grad_attn, ssm_input, ssm_b, ssm_c, log_decay, skip_gain, grad_ssm, doc_lengths):
        tok, kw = keys.shape
        width, state = ssm_input.shape[1], ssm_b.shape[1]
        ratio = queries.shape[1] // kw
        groups = kw // D_HEAD
        share = tok // ways
        vmem = pl.BlockSpec(memory_space=pltpu.VMEM)
        hbm = pl.BlockSpec(memory_space=pltpu.HBM)
        held = lambda a: pltpu.VMEM(a.shape, a.dtype)
        skips, lens = skip_gain.reshape(1, -1), doc_lengths.reshape(1, -1)
        shapes = [queries.shape, keys.shape, values.shape, ssm_input.shape, (share, state), (share, state)]
        results = pl.pallas_call(
            lambda *refs: kernel(shards, ways, *refs),
            out_shape=tuple(jax.ShapeDtypeStruct(shape, BF16) for shape in shapes),
            in_specs=[hbm] * 11,
            out_specs=(vmem,) * 6,
            scratch_shapes=[
                held(queries),
                held(grad_attn),
                held(ssm_input),
                held(ssm_b),
                held(log_decay),
                held(skips),
                held(grad_ssm),
                held(lens),
                pltpu.VMEM((groups, SLOTS * tok, 2 * D_HEAD), BF16),
                pltpu.VMEM((SLOTS * tok, width // 2 + state), BF16),
                pltpu.VMEM((SLOTS * 8, width // 8), F32),
                pltpu.VMEM((SLOTS * tok, width // 2), BF16),
                pltpu.VMEM((SLOTS * tok, width // 2), BF16),
                pltpu.VMEM((SLOTS * tok, state), BF16),
                pltpu.VMEM((SLOTS * 8, width // 8), F32),
                pltpu.VMEM((tok, width), BF16),
                pltpu.VMEM((groups, SLOTS * tok, 2 * D_HEAD), F32),
                pltpu.VMEM((groups, 3 * tok, 2 * D_HEAD), BF16),
                pltpu.VMEM((groups, 3 * tok, 2 * D_HEAD), BF16),
                pltpu.VMEM((groups, tok, 2 * D_HEAD), BF16),
                pltpu.VMEM((groups, tok, 2 * D_HEAD), BF16),
                pltpu.VMEM((groups, tok, 2 * D_HEAD), BF16),
                pltpu.VMEM((groups, tok, 2 * D_HEAD), BF16),
                pltpu.VMEM(((REACH + 1) * tok, ratio * tok), BF16),
                pltpu.VMEM(((REACH + 1) * tok, ratio * tok), BF16),
                pltpu.VMEM((tok, width), F32),
                pltpu.VMEM((tok, width), F32),
                pltpu.VMEM((state, width), F32),
                pltpu.VMEM((2 * tok, state), F32),
                pltpu.VMEM((ways, 2 * share, state), BF16),
                pltpu.VMEM((ways - 1, 2 * share, state), BF16),
                pltpu.VMEM((2 * tok, state), F32),
                pltpu.VMEM((ways, 2 * share, state), BF16),
                pltpu.VMEM((ways - 1, 2 * share, state), BF16),
                pltpu.VMEM((2 * tok, state), F32),
                pltpu.VMEM((ways, 2 * share, state), BF16),
                pltpu.VMEM((ways - 1, 2 * share, state), BF16),
                pltpu.VMEM((REACH, share, state), BF16),
                pltpu.VMEM((REACH, share, state), BF16),
                pltpu.SemaphoreType.DMA((TRANSFERS,)),
                pltpu.SemaphoreType.DMA((TRANSFERS,)),
                pltpu.SemaphoreType.DMA((9 + 2 * groups,)),
                pltpu.SemaphoreType.REGULAR,
            ],
            compiler_params=pltpu.CompilerParams(
                collective_id=0, has_side_effects=True, vmem_limit_bytes=VMEM_BYTES
            ),
        )(
            queries,
            keys,
            values,
            grad_attn,
            ssm_input,
            ssm_b,
            ssm_c,
            log_decay,
            skips,
            grad_ssm,
            lens,
        )
        return pl.pallas_call(
            hand_over,
            out_shape=tuple(jax.ShapeDtypeStruct(shape, BF16) for shape in shapes),
            in_specs=[vmem] * 6,
            out_specs=(vmem,) * 6,
        )(*results)

    both = P("ctx", "head")
    rows = P(("ctx", "head"), None)
    return jax.shard_map(
        on_device,
        mesh=mesh,
        in_specs=(both, both, both, both, both, P("ctx", None), P("ctx", None), P("head", "ctx"), P("head"), both, P()),
        out_specs=(both, both, both, both, rows, rows),
        check_vma=False,
    )
```

time: 55.4 us -> 42.9 us (0.77)
  local copies, waits for them, and re-layouts: 12.4 us -> 0 us
    unnamed x28 -> x0, local copies, waits for them, and re-layouts: 12.4 us -> none
    pallas_call x1 -> x2, Pallas kernels: 41.9 us -> 42.1 us  [the longest x1 40.2 us: on_device(): pl.pallas_call(lambda *refs: kernel(shards, ways, *refs), out_shape=tuple...]
where the time goes in v2:
time: 42.9 us; the launch traced here: 42.8 us
  Pallas kernels  42.1 us (98%)
  between operations  0.64 us (1%)
    pallas_call x1, Pallas kernels, on_device(): pl.pallas_call(lambda *refs: kernel(shards, ways, *refs), out_shape=tuple...  40.2 us
    pallas_call x1, Pallas kernels, on_device(): pl.pallas_call(hand_over, out_shape=tuple((jax.ShapeDtypeStruct(shape, BF...  1.91 us

profile of v2, /device:TPU:1, one launch (start us, length us, event | category | flops | bytes accessed | tf_op | source)
XLA Modules:
  0.0 42.8 jit_solution(6776169637727742165)
XLA Ops:
  0.6 40.2 %shard_map.154 = (bf16[128,1024]{1,0:T(8,128)(2,1)}, bf16[128,256]{1,0:T(8,128)(2,1)}, bf16[128,256]{1,0:T(8,128)(2,1)}, bf16[128,1024]{1,0:T(8,128)(2,1)}, bf16...) custom-call(bf16[128,1024]{1,0:T(8,128)(2,1)} %refs_0_.1, bf16[128,256]{1,0:T(8,128)(2,1)} %refs_1_.1, ...), custom_call_target="tpu_custom_call" | custom-call | tf_op jit(solution)/shard_map/pallas_call | solution.py:535
  40.8 1.9 %shard_map.155 = (bf16[128,1024]{1,0:T(8,128)(2,1)}, bf16[128,256]{1,0:T(8,128)(2,1)}, bf16[128,256]{1,0:T(8,128)(2,1)}, bf16[128,1024]{1,0:T(8,128)(2,1)}, bf16...) custom-call(bf16[128,1024]{1,0:T(8,128)(2,1)} %get-tuple-element.12.refs_0_, bf16[128,256]{1,0:T(8,128)(2,1)} %get-tuple-element.13.refs_1_, ...), custom_call_target="tpu_custom_call" | custom-call | tf_op jit(solution)/shard_map/pallas_call | solution.py:601

commit v3 on v2

--- a/solution.py
+++ b/solution.py
@@ -126,7 +126,7 @@
     up, down = along(2), along(-2)
     others = [(shard, lax.rem(way + j, ways)) for j in range(1, ways)]
     barrier = pltpu.get_barrier_semaphore()
-    for peer in [along(-k) for k in range(1, REACH + 1)] + [mate] + others:
+    for peer in [along(-1), along(-2), mate] + others:
         pl.semaphore_signal(barrier, inc=1, device_id=peer, device_id_type=MESH)
 
     def rows(slot, size=tok):
@@ -236,60 +236,58 @@
             for one in loads[name]:
                 one.wait()
 
-    loaded("lens", "decay", "skip")
-    base = shard * tok
-    start_col, start_row = document_starts(lens_ref[...], base, tok)
-    decay = decay_ref[...]
-    later = (iota((tok, tok), 0) >= iota((tok, tok), 1)).astype(F32)
-    cum_col = dot(later, decay, (1, 1), HIGH)
-    cum_row = dot(decay, later, (1, 1), HIGH)
-    total = cum_col[tok - 1 : tok, :]
-    base_f = base.astype(F32)
-    last_start = start_col[tok - 1 : tok, :]
-    ending = jnp.exp(total - cum_col) * (start_col == last_start).astype(F32)
-    carried = jnp.exp(cum_col) * (start_col < base_f).astype(F32)
-    through = jnp.exp(total) * (last_start < base_f).astype(F32)
-    table = jnp.concatenate(
-        [ending, carried, jnp.broadcast_to(through, (8, heads)), jnp.broadcast_to(skip_ref[...], (8, heads))],
-        axis=0,
-    )
-    spread = (iota((heads, width), 1) // MDIM == iota((heads, width), 0)).astype(BF16)
-    table_hi = table.astype(BF16)
-    table_mid = (table - table_hi.astype(F32)).astype(BF16)
-    table_lo = (table - table_hi.astype(F32) - table_mid.astype(F32)).astype(BF16)
-    wide = dot(table_hi, spread, (1, 0)) + dot(table_mid, spread, (1, 0)) + dot(table_lo, spread, (1, 0))
-    skip = wide[2 * tok + 8 : 2 * tok + 9]
-    th = jnp.concatenate(
-        [wide[2 * tok : 2 * tok + 1, i * (width // 8) : (i + 1) * (width // 8)] for i in range(8)], axis=0
-    )
-    bth[rows(core, 8)] = th
-    fth[rows(4 + core, 8)] = th
-    to_end[...] = wide[0:tok]
-
+    def pieces(value):
+        high = value.astype(BF16)
+        middle = (value - high.astype(F32)).astype(BF16)
+        return high, middle, (value - high.astype(F32) - middle.astype(F32)).astype(BF16)
+
+    def widen(value, count):
+        return sum(dot(piece, spread, (1, 0)) for piece in pieces(value)[:count])
+
+    pl.semaphore_wait(barrier, 3 + len(others))
+    pl.semaphore_signal(ready, inc=1, device_id=up, device_id_type=MESH)
     loaded("k", "v")
-    pl.semaphore_wait(barrier, REACH + 1 + len(others))
-    pl.semaphore_signal(ready, inc=1, device_id=up, device_id_type=MESH)
     for halo in kv_halos:
         halo.begin()
     for halo in kv_halos:
         halo.begin_mate()
+    loaded("lens", "decay", "skip")
+    base = shard * tok
+    base_f = base.astype(F32)
+    start_col, start_row = document_starts(lens_ref[...], base, tok)
+    later = (iota((tok, tok), 0) >= iota((tok, tok), 1)).astype(BF16)
+    decay_pieces = pieces(decay_ref[...])
+    cum_col = sum(dot(later, piece, (1, 1)) for piece in decay_pieces)
+    carried = jnp.exp(cum_col) * (start_col < base_f).astype(F32)
+    spread = (iota((heads, width), 1) // MDIM == iota((heads, width), 0)).astype(BF16)
+    total = cum_col[tok - 1 : tok, :]
+    last_start = start_col[tok - 1 : tok, :]
+    through = jnp.exp(total) * (last_start < base_f).astype(F32)
+    table = jnp.concatenate([jnp.broadcast_to(through, (8, heads)), jnp.broadcast_to(skip_ref[...], (8, heads))], axis=0)
+    wide = widen(table, 3)
+    skip = wide[8:9]
+    th = jnp.concatenate([wide[0:1, i * (width // 8) : (i + 1) * (width // 8)] for i in range(8)], axis=0)
+    bth[rows(core, 8)] = th
+    fth[rows(4 + core, 8)] = th
+    fth_halo.begin()
+    wide = widen(carried, 2)
     loaded("g", "c")
-    scaled = (g_ref[...].astype(F32) * wide[tok : 2 * tok]).astype(BF16)
-    ga[g_own] = scaled[:, 0:half]
-    gb[g_own] = scaled[:, half:]
+    ga[g_own] = (g_ref[:, 0:half].astype(F32) * wide[:, 0:half]).astype(BF16)
+    gb[g_own] = (g_ref[:, half:].astype(F32) * wide[:, half:]).astype(BF16)
     pl.semaphore_wait(ready, 1)
     put(c_part(core, way), c_part(2 + core, way), down, ("c", "near"))
     bth_halo.begin()
     ga_halo.begin()
     gb_halo.begin()
+    to_end[...] = widen(jnp.exp(total - cum_col) * (start_col == last_start).astype(F32), 2)
     loaded("x", "b")
-    xs[...] = (x_ref[...].astype(F32) * wide[0:tok]).astype(BF16)
+    xs[...] = (x_ref[...].astype(F32) * to_end[...]).astype(BF16)
     fx[own, 0:half] = xs[:, half:]
     fx[own, half:] = b_ref[...]
-    fth_halo.begin()
     for halo in (fth_halo, bth_halo, ga_halo, gb_halo, x_halo):
         halo.begin_mate()
     put(bc.at[g_own], bc.at[g_own], mate, ("c", "mate", "own"))
+    cum_row = sum(dot(piece, later, (1, 1)) for piece in decay_pieces)
     state = dot(b_ref[...], xs[:, 0:half], (0, 0))
 
     causal = (iota((tok, tok), 0) >= iota((tok, tok), 1)) & (
@@ -450,16 +448,9 @@
     early[0:tok] = ahead(1, None)
     early[tok : 2 * tok] = ahead(2, th1)
     sum_start(early, early_out, early_in, "early", 0, 2)
-    send_far(groups - 1)
     ga_halo.finish()
     bth_halo.finish()
-    fth_halo.finish()
-    c_gather(4 + core, "far")
-    arrived(bc.at[rows(1 - core)], ("c", "mate", "own"))
-    arrived(bc.at[rows(3 - core)], ("c", "mate", "near"))
-    near_adjoint[:, first_half] = adjoint_of(ga, 1) + th1[:, first_half] * adjoint_of(ga, 2)
-    gb_halo.wait_near()
-    near_adjoint[:, second_half] = adjoint_of(gb, 1) + th1[:, second_half] * adjoint_of(gb, 2)
+    send_far(groups - 1)
     bth_halo.wait_far()
     th2 = th1 * decay_through(bth, core + 2)
     th3 = decay_through(bth, core + 3)
@@ -467,12 +458,20 @@
     late[0:tok] = ahead(3, th2)
     late[tok : 2 * tok] = ahead(4, th2 * th3)
     sum_start(late, late_out, late_in, "late", 0, 2)
+    x_halo.finish()
+    fth_halo.finish()
+    gb_halo.finish()
+    c_gather(4 + core, "far")
+    arrived(bc.at[rows(1 - core)], ("c", "mate", "own"))
+    arrived(bc.at[rows(3 - core)], ("c", "mate", "near"))
+    near_adjoint[:, first_half] = adjoint_of(ga, 1) + th1[:, first_half] * adjoint_of(ga, 2)
+    gb_halo.wait_near()
+    near_adjoint[:, second_half] = adjoint_of(gb, 1) + th1[:, second_half] * adjoint_of(gb, 2)
     ahead_1, ahead_2 = sum_finish(early, early_in, "early", 0, 2)
     send_ahead(1, ahead_1)
     send_ahead(2, ahead_2)
     for group in range(groups):
         send_near(group)
-    x_halo.finish()
     arrived(bc.at[rows(5 - core)], ("c", "mate", "far"))
 
     def adjoint(ref, part):
@@ -483,7 +482,6 @@
     ahead_3, ahead_4 = sum_finish(late, late_in, "late", 0, 2)
     send_ahead(3, ahead_3)
     send_ahead(4, ahead_4)
-    gb_halo.finish()
 
     x_halo.wait_near()
     fth_halo.wait_near()
@@ -534,7 +532,7 @@
         shapes = [queries.shape, keys.shape, values.shape, ssm_input.shape, (share, state), (share, state)]
         results = pl.pallas_call(
             lambda *refs: kernel(shards, ways, *refs),
-            out_shape=tuple(jax.ShapeDtypeStruct(shape, BF16) for shape in shapes),
+            out_shape=tuple(pltpu.VMEM(shape, BF16) for shape in shapes),
             in_specs=[hbm] * 11,
             out_specs=(vmem,) * 6,
             scratch_shapes=[
@@ -603,6 +601,7 @@
             out_shape=tuple(jax.ShapeDtypeStruct(shape, BF16) for shape in shapes),
             in_specs=[vmem] * 6,
             out_specs=(vmem,) * 6,
+            compiler_params=pltpu.CompilerParams(vmem_limit_bytes=4 * 1024 * 1024),
         )(*results)
 
     both = P("ctx", "head")

time: 42.9 us -> 38.9 us (0.907)
  Pallas kernels: 42.1 us -> 38.2 us
    pallas_call x1, Pallas kernels: 40.2 us -> 37.3 us  [on_device(): pl.pallas_call(lambda *refs: kernel(shards, ways, *refs), out_shape=tuple...]
    pallas_call x1, Pallas kernels: 1.91 us -> 0.87 us  [on_device(): pl.pallas_call(hand_over, out_shape=tuple((jax.ShapeDtypeStruct(shape, BF...]
where the time goes in v3:
time: 38.9 us; the launch traced here: 38.8 us
  Pallas kernels  38.2 us (98%)
  between operations  0.64 us (2%)
    pallas_call x1, Pallas kernels, on_device(): pl.pallas_call(lambda *refs: kernel(shards, ways, *refs), out_shape=tuple...  37.3 us
    pallas_call x1, Pallas kernels, on_device(): pl.pallas_call(hand_over, out_shape=tuple((jax.ShapeDtypeStruct(shape, BF...  0.87 us

profile of v3, /device:TPU:1, one launch (start us, length us, event | category | flops | bytes accessed | tf_op | source)
XLA Modules:
  0.0 38.8 jit_solution(5706713948818037890)
XLA Ops:
  0.6 37.3 %shard_map.154 = (bf16[128,1024]{1,0:T(8,128)(2,1)S(1)}, bf16[128,256]{1,0:T(8,128)(2,1)S(1)}, bf16[128,256]{1,0:T(8,128)(2,1)S(1)}, bf16[128,1024]{1,0:T(8,128)...) custom-call(bf16[128,1024]{1,0:T(8,128)(2,1)} %refs_0_.1, bf16[128,256]{1,0:T(8,128)(2,1)} %refs_1_.1, ...), custom_call_target="tpu_custom_call" | custom-call | tf_op jit(solution)/shard_map/pallas_call | solution.py:533
  37.9 0.9 %shard_map.155 = (bf16[128,1024]{1,0:T(8,128)(2,1)}, bf16[128,256]{1,0:T(8,128)(2,1)}, bf16[128,256]{1,0:T(8,128)(2,1)}, bf16[128,1024]{1,0:T(8,128)(2,1)}, bf16...) custom-call(bf16[128,1024]{1,0:T(8,128)(2,1)S(1)} %get-tuple-element.12.refs_0_, ...), custom_call_target="tpu_custom_call" | custom-call | tf_op jit(solution)/shard_map/pallas_call | solution.py:599

commit v4 on v3

--- a/solution.py
+++ b/solution.py
@@ -11,6 +11,7 @@
 MDIM = 64
 REACH = 4
 SLOTS = REACH + 2
+EIGHTHS = 5
 TRANSFERS = 72
 VMEM_BYTES = 56 * 1024 * 1024
 
@@ -114,7 +115,8 @@
     ratio = q_ref.shape[1] // kw
     width = x_ref.shape[1]
     share = tok // ways
-    half = width // 2
+    half = width // 8 * EIGHTHS
+    rest = width - half
     shard = lax.axis_index("ctx")
     way = lax.axis_index("head")
     core = lax.rem(shard, 2)
@@ -282,8 +284,8 @@
     to_end[...] = widen(jnp.exp(total - cum_col) * (start_col == last_start).astype(F32), 2)
     loaded("x", "b")
     xs[...] = (x_ref[...].astype(F32) * to_end[...]).astype(BF16)
-    fx[own, 0:half] = xs[:, half:]
-    fx[own, half:] = b_ref[...]
+    fx[own, 0:rest] = xs[:, half:]
+    fx[own, rest:] = b_ref[...]
     for halo in (fth_halo, bth_halo, ga_halo, gb_halo, x_halo):
         halo.begin_mate()
     put(bc.at[g_own], bc.at[g_own], mate, ("c", "mate", "own"))
@@ -490,7 +492,7 @@
     state_in = None
     for k in range(REACH, 0, -1):
         place = 4 + core - k
-        value = dot(fx[rows(place), half:], fx[rows(place), 0:half], (0, 0))
+        value = dot(fx[rows(place), rest:], fx[rows(place), 0:rest], (0, 0))
         state_in = value if state_in is None else value + decay_through(fth, place)[:, half:] * state_in
     last[tok : 2 * tok] = last[tok : 2 * tok] + dot(gb[g_own], state_in.astype(BF16), (1, 1))
     sum_start(last, last_out, last_in, "last", 1, 2)
@@ -545,10 +547,10 @@
                 held(grad_ssm),
                 held(lens),
                 pltpu.VMEM((groups, SLOTS * tok, 2 * D_HEAD), BF16),
-                pltpu.VMEM((SLOTS * tok, width // 2 + state), BF16),
+                pltpu.VMEM((SLOTS * tok, width // 8 * (8 - EIGHTHS) + state), BF16),
                 pltpu.VMEM((SLOTS * 8, width // 8), F32),
-                pltpu.VMEM((SLOTS * tok, width // 2), BF16),
-                pltpu.VMEM((SLOTS * tok, width // 2), BF16),
+                pltpu.VMEM((SLOTS * tok, width // 8 * EIGHTHS), BF16),
+                pltpu.VMEM((SLOTS * tok, width // 8 * (8 - EIGHTHS)), BF16),
                 pltpu.VMEM((SLOTS * tok, state), BF16),
                 pltpu.VMEM((SLOTS * 8, width // 8), F32),
                 pltpu.VMEM((tok, width), BF16),

time: 38.9 us -> 38.4 us (0.987)
  Pallas kernels: 38.2 us -> 37.7 us
    pallas_call x1, Pallas kernels: 37.3 us -> 36.8 us  [on_device(): pl.pallas_call(lambda *refs: kernel(shards, ways, *refs), out_shape=tuple...]
where the time goes in v4:
time: 38.4 us; the launch traced here: 38.3 us
  Pallas kernels  37.7 us (98%)
  between operations  0.64 us (2%)
    pallas_call x1, Pallas kernels, on_device(): pl.pallas_call(lambda *refs: kernel(shards, ways, *refs), out_shape=tuple...  36.8 us
    pallas_call x1, Pallas kernels, on_device(): pl.pallas_call(hand_over, out_shape=tuple((jax.ShapeDtypeStruct(shape, BF...  0.87 us

profile of v4, /device:TPU:1, one launch (start us, length us, event | category | flops | bytes accessed | tf_op | source)
XLA Modules:
  0.0 38.3 jit_solution(7538243920442352686)
XLA Ops:
  0.6 36.8 %shard_map.154 = (bf16[128,1024]{1,0:T(8,128)(2,1)S(1)}, bf16[128,256]{1,0:T(8,128)(2,1)S(1)}, bf16[128,256]{1,0:T(8,128)(2,1)S(1)}, bf16[128,1024]{1,0:T(8,128)...) custom-call(bf16[128,1024]{1,0:T(8,128)(2,1)} %refs_0_.1, bf16[128,256]{1,0:T(8,128)(2,1)} %refs_1_.1, ...), custom_call_target="tpu_custom_call" | custom-call | tf_op jit(solution)/shard_map/pallas_call | solution.py:535
  37.4 0.9 %shard_map.155 = (bf16[128,1024]{1,0:T(8,128)(2,1)}, bf16[128,256]{1,0:T(8,128)(2,1)}, bf16[128,256]{1,0:T(8,128)(2,1)}, bf16[128,1024]{1,0:T(8,128)(2,1)}, bf16...) custom-call(bf16[128,1024]{1,0:T(8,128)(2,1)S(1)} %get-tuple-element.12.refs_0_, ...), custom_call_target="tpu_custom_call" | custom-call | tf_op jit(solution)/shard_map/pallas_call | solution.py:601

commit v5 on v4

--- a/solution.py
+++ b/solution.py
@@ -472,6 +472,9 @@
     ahead_1, ahead_2 = sum_finish(early, early_in, "early", 0, 2)
     send_ahead(1, ahead_1)
     send_ahead(2, ahead_2)
+    ahead_3, ahead_4 = sum_finish(late, late_in, "late", 0, 2)
+    send_ahead(3, ahead_3)
+    send_ahead(4, ahead_4)
     for group in range(groups):
         send_near(group)
     arrived(bc.at[rows(5 - core)], ("c", "mate", "far"))
@@ -481,9 +484,6 @@
         return (near_adjoint[:, part] + th2[:, part] * far).astype(BF16)
 
     finish_input(first_half, adjoint(ga, first_half))
-    ahead_3, ahead_4 = sum_finish(late, late_in, "late", 0, 2)
-    send_ahead(3, ahead_3)
-    send_ahead(4, ahead_4)
 
     x_halo.wait_near()
     fth_halo.wait_near()

time: 38.4 us -> 38.1 us (level)
  no operation moved by 1% of the time
where the time goes in v5:
time: 38.1 us; the launch traced here: 38 us
  Pallas kernels  37.4 us (98%)
  between operations  0.64 us (2%)
    pallas_call x1, Pallas kernels, on_device(): pl.pallas_call(lambda *refs: kernel(shards, ways, *refs), out_shape=tuple...  36.5 us
    pallas_call x1, Pallas kernels, on_device(): pl.pallas_call(hand_over, out_shape=tuple((jax.ShapeDtypeStruct(shape, BF...  0.87 us

profile of v5, /device:TPU:1, one launch (start us, length us, event | category | flops | bytes accessed | tf_op | source)
XLA Modules:
  0.0 38.0 jit_solution(9641763775960368867)
XLA Ops:
  0.6 36.5 %shard_map.154 = (bf16[128,1024]{1,0:T(8,128)(2,1)S(1)}, bf16[128,256]{1,0:T(8,128)(2,1)S(1)}, bf16[128,256]{1,0:T(8,128)(2,1)S(1)}, bf16[128,1024]{1,0:T(8,128)...) custom-call(bf16[128,1024]{1,0:T(8,128)(2,1)} %refs_0_.1, bf16[128,256]{1,0:T(8,128)(2,1)} %refs_1_.1, ...), custom_call_target="tpu_custom_call" | custom-call | tf_op jit(solution)/shard_map/pallas_call | solution.py:535
  37.2 0.9 %shard_map.155 = (bf16[128,1024]{1,0:T(8,128)(2,1)}, bf16[128,256]{1,0:T(8,128)(2,1)}, bf16[128,256]{1,0:T(8,128)(2,1)}, bf16[128,1024]{1,0:T(8,128)(2,1)}, bf16...) custom-call(bf16[128,1024]{1,0:T(8,128)(2,1)S(1)} %get-tuple-element.12.refs_0_, ...), custom_call_target="tpu_custom_call" | custom-call | tf_op jit(solution)/shard_map/pallas_call | solution.py:601

commit v6 on v5

--- a/solution.py
+++ b/solution.py
@@ -499,6 +499,9 @@
     gb_halo.wait_far()
     finish_input(second_half, adjoint(gb, second_half))
     sum_start(last, last_out, last_in, "last", 0, 1)
+    recent = 16
+    for one in started[:-recent]:
+        one.wait_send()
     for group in range(groups):
         finish_keys(group)
     (sum_c,) = sum_finish(last, last_in, "last", 1, 2)
@@ -508,7 +511,7 @@
     dc_ref[...] = sum_c.astype(BF16)
     (sum_b,) = sum_finish(last, last_in, "last", 0, 1)
     db_ref[...] = sum_b.astype(BF16)
-    for one in started:
+    for one in started[-recent:]:
         one.wait_send()
 
 

time: 38.1 us -> 38 us (level)
  no operation moved by 1% of the time
where the time goes in v6:
time: 38 us
  Pallas kernels  37.3 us (98%)
  between operations  0.64 us (2%)
    pallas_call x1, Pallas kernels, on_device(): pl.pallas_call(lambda *refs: kernel(shards, ways, *refs), out_shape=tuple...  36.4 us
    pallas_call x1, Pallas kernels, on_device(): pl.pallas_call(hand_over, out_shape=tuple((jax.ShapeDtypeStruct(shape, BF...  0.87 us

profile of v6, /device:TPU:1, one launch (start us, length us, event | category | flops | bytes accessed | tf_op | source)
XLA Modules:
  0.0 38.0 jit_solution(44588711297578271)
XLA Ops:
  0.6 36.4 %shard_map.154 = (bf16[128,1024]{1,0:T(8,128)(2,1)S(1)}, bf16[128,256]{1,0:T(8,128)(2,1)S(1)}, bf16[128,256]{1,0:T(8,128)(2,1)S(1)}, bf16[128,1024]{1,0:T(8,128)...) custom-call(bf16[128,1024]{1,0:T(8,128)(2,1)} %refs_0_.1, bf16[128,256]{1,0:T(8,128)(2,1)} %refs_1_.1, ...), custom_call_target="tpu_custom_call" | custom-call | tf_op jit(solution)/shard_map/pallas_call | solution.py:538
  37.1 0.9 %shard_map.155 = (bf16[128,1024]{1,0:T(8,128)(2,1)}, bf16[128,256]{1,0:T(8,128)(2,1)}, bf16[128,256]{1,0:T(8,128)(2,1)}, bf16[128,1024]{1,0:T(8,128)(2,1)}, bf16...) custom-call(bf16[128,1024]{1,0:T(8,128)(2,1)S(1)} %get-tuple-element.12.refs_0_, ...), custom_call_target="tpu_custom_call" | custom-call | tf_op jit(solution)/shard_map/pallas_call | solution.py:604
